TPU v7x, 512 devices: a whole 4x4x16 slice. The times are simulated.
512 devices in a mesh: tensor: 16 (over z_lo, y), context: 32 (over x, z_hi, core).
Axes of the slice: x: 4, y: 4, z: 16 (z_hi: 4, z_lo: 4; z = z_hi * 4 + z_lo), core: 2. Of those that a mesh axis runs over, the one named last changes fastest.
Arguments:
- sequence: bfloat16 [2, 1024, 16384], P(None, 'tensor', 'context'), may hold values from -6 to 6
- gate: bfloat16 [2, 1024, 16384], P(None, 'tensor', 'context'), may hold values from -6 to 6
- skip: float32 [1024], P('tensor'), may hold values from -4 to 4
- filter_spectrum: float32 [2, 1024, 64, 512], P(None, 'tensor', 'context'), may hold values from -6 to 6
- out_weight: bfloat16 [1024, 4096], P(None, 'tensor'), may hold values from -0.1875 to 0.1875
Outputs:
- projected: bfloat16 [2, 16384, 4096], P(None, 'context', 'tensor')
All inputs are finite; a program needn't handle non-finite values.
Results may differ from a plain program's by a relative error of at most 0.0049.
Values may be sent and summed in bfloat16 or wider, within the bound.
A program may use at most 64 MiB of HBM per device.

v0:
```python
import math

import jax
import jax.numpy as jnp
from jax import lax
from jax.sharding import PartitionSpec as P

precise = lax.Precision.HIGHEST


def phase_table(left_idx, right_idx, period):
    turns = left_idx * right_idx % period
    angle = turns.astype(jnp.float32) * (2.0 * math.pi / period)
    return (jnp.cos(angle), jnp.sin(angle))


def inner_forward(col_re, col_im, cos_b, sin_b):
    freq_re = jnp.einsum("sgqb,bk->sgqk", col_re, cos_b, precision=precise) + jnp.einsum(
        "sgqb,bk->sgqk", col_im, sin_b, precision=precise
    )
    freq_im = jnp.einsum("sgqb,bk->sgqk", col_im, cos_b, precision=precise) - jnp.einsum(
        "sgqb,bk->sgqk", col_re, sin_b, precision=precise
    )
    return (freq_re, freq_im)


def inner_filtered(freq_re, freq_im, spec_re, spec_im, cos_b, sin_b):
    prod_re = freq_re * spec_re - freq_im * spec_im
    prod_im = freq_re * spec_im + freq_im * spec_re
    back_re = jnp.einsum("sgqk,kb->sgqb", prod_re, cos_b, precision=precise) - jnp.einsum(
        "sgqk,kb->sgqb", prod_im, sin_b, precision=precise
    )
    back_im = jnp.einsum("sgqk,kb->sgqb", prod_im, cos_b, precision=precise) + jnp.einsum(
        "sgqk,kb->sgqb", prod_re, sin_b, precision=precise
    )
    return (back_re, back_im)


def convolve_group(inputs, spectrum):
    num_seqs, group_ch, block_len = inputs.shape
    peers = lax.axis_size("context")
    my_index = lax.axis_index("context")
    slice_len = block_len // peers
    freq_rows = 2 * peers
    fft_len = freq_rows * block_len
    blocks = lax.all_to_all(
        inputs.reshape(num_seqs, group_ch, peers, slice_len),
        "context",
        split_axis=2,
        concat_axis=2,
        tiled=True,
    )
    blocks = blocks.astype(jnp.float32)
    source = jnp.arange(peers, dtype=jnp.int32)
    residue = jnp.arange(freq_rows, dtype=jnp.int32)
    cos_c, sin_c = phase_table(source[:, None], residue[None, :], freq_rows)
    real_part = jnp.einsum("sgcb,ck->sgkb", blocks, cos_c, precision=precise)
    imag_part = -jnp.einsum("sgcb,ck->sgkb", blocks, sin_c, precision=precise)
    local_pos = my_index * slice_len + jnp.arange(slice_len, dtype=jnp.int32)
    cos_t, sin_t = phase_table(residue[:, None], local_pos[None, :], fft_len)
    turned = jnp.stack(
        [real_part * cos_t + imag_part * sin_t, imag_part * cos_t - real_part * sin_t]
    )
    columns = lax.all_to_all(turned, "context", split_axis=3, concat_axis=4, tiled=True)
    position = jnp.arange(block_len, dtype=jnp.int32)
    cos_b, sin_b = phase_table(position[:, None], position[None, :], block_len)
    freq_re, freq_im = inner_forward(columns[0], columns[1], cos_b, sin_b)
    back_re, back_im = inner_filtered(
        freq_re, freq_im, spectrum[0][None], spectrum[1][None], cos_b, sin_b
    )
    own_residue = 2 * my_index + jnp.arange(2, dtype=jnp.int32)
    cos_i, sin_i = phase_table(own_residue[:, None], position[None, :], fft_len)
    rotated = jnp.stack([back_re * cos_i - back_im * sin_i, back_im * cos_i + back_re * sin_i])
    returned = lax.all_to_all(rotated, "context", split_axis=4, concat_axis=3, tiled=True)
    cos_o, sin_o = phase_table(residue[:, None], source[None, :], freq_rows)
    signal = jnp.einsum("sgkb,kc->sgcb", returned[0], cos_o, precision=precise) - jnp.einsum(
        "sgkb,kc->sgcb", returned[1], sin_o, precision=precise
    )
    signal = signal * (1.0 / fft_len)
    gathered = lax.all_to_all(signal, "context", split_axis=2, concat_axis=3, tiled=True)
    return gathered.reshape(num_seqs, group_ch, block_len)


def local(sequence, gate, skip, filter_spectrum, out_weight):
    num_seqs, local_ch, block_len = sequence.shape
    tensor_count = lax.axis_size("tensor")
    group_count = 1
    group_ch = local_ch // group_count
    out_cols = out_weight.shape[1]
    weight_groups = out_weight.reshape(tensor_count, group_count, group_ch, out_cols)
    running_sum = jnp.zeros((num_seqs, block_len, out_cols), jnp.float32)
    convolved = convolve_group(sequence, filter_spectrum)
    mixed = (
        gate.astype(jnp.float32) * (convolved + skip[None, :, None] * sequence.astype(jnp.float32))
    ).astype(jnp.bfloat16)
    weight_rows = weight_groups[:, 0].reshape(tensor_count * group_ch, out_cols)

    def accumulate(partial_sum, shard_rows, first_row, weight_rows=weight_rows):
        return jnp.einsum(
            "sdt,do->sto", shard_rows, weight_rows, preferred_element_type=jnp.float32
        )

    running_sum = accumulate(
        running_sum, lax.all_gather(mixed, "tensor", axis=1, tiled=True), jnp.int32(0)
    )
    return running_sum.astype(jnp.bfloat16)


def solution(mesh):
    in_specs = (
        P(None, "tensor", "context"),
        P(None, "tensor", "context"),
        P("tensor"),
        P(None, "tensor", "context", None),
        P(None, "tensor"),
    )
    out_specs = P(None, "context", "tensor")
    return jax.shard_map(local, mesh=mesh, in_specs=in_specs, out_specs=out_specs, check_vma=False)
```

profile of v0, /device:TPU:2, one launch (start us, length us, event | category | flops | bytes accessed | tf_op | source)
XLA Modules:
  0.0 364.9 jit_solution(301034999238765829)
XLA Ops:
  8.5 18.2 %all-to-all-start = ((bf16[32,2,1024]{2,1,0:T(2,128)(2,1)}), bf16[32,2,1024]{2,1,0:T(2,128)(2,1)S(1)}, u32[]{:S(2)}, u32[]{:S(2)}) async-start(bf16[32,2,1024]{2,1,0:T(2,128)(2,1)} %reshape.140), calls=%async_computation | async-start | bytes 262144 | tf_op jit(solution)/shard_map/all_to_all | solution.py:46
  26.9 14.2 %all-to-all-done = bf16[32,2,1024]{2,1,0:T(2,128)(2,1)S(1)} async-done(((bf16[32,2,1024]{2,1,0:T(2,128)(2,1)}), bf16[32,2,1024]{2,1,0:T(2,128)(2,1)S(1)}, u32[]{:S(2)}, u32[]{:S(2)}) %all-to-all-start) | async-done | bytes 131104 | tf_op jit(solution)/shard_map/all_to_all | solution.py:46
  44.7 2.3 reshape.142
  47.0 6.9 %all-to-all-start.1 = ((f32[32,1,8192]{2,1,0:T(1,128)}), f32[32,1,8192]{2,1,0:T(1,128)S(1)}, u32[]{:S(2)}, u32[]{:S(2)}) async-start(f32[32,1,8192]{2,1,0:T(1,128)} %reshape.142), calls=%async_computation.1 | async-start | bytes 2097152 | tf_op jit(solution)/shard_map/all_to_all | solution.py:64
  54.3 33.2 %all-to-all-done.1 = f32[32,1,8192]{2,1,0:T(1,128)S(1)} async-done(((f32[32,1,8192]{2,1,0:T(1,128)}), f32[32,1,8192]{2,1,0:T(1,128)S(1)}, u32[]{:S(2)}, u32[]{:S(2)}) %all-to-all-start.1) | async-done | bytes 1048608 | tf_op jit(solution)/shard_map/all_to_all | solution.py:64
  88.0 4.4 %reduce = f32[32,8192]{1,0:T(8,128)} reduce(f32[32,1,8192]{2,1,0:T(1,128)S(1)} %all-to-all-done.1, f32[]{:T(128)} %broadcast.231), dimensions={1}, to_apply=%all_to_all.33.reduce_sub_computation | reduce | bytes 2097156 | tf_op jit(solution)/shard_map/all_to_all | solution.py:64
  92.4 2.2 reshape.143
  94.9 7.0 %fusion.15 = f32[2,64,2,512]{3,1,2,0:T(8,128)S(1)} fusion(f32[2,64,2,512]{1,3,2,0:T(8,128)S(1)} %bitcast.114), kind=kOutput, calls=%fused_computation.28 | convolution fusion | flops 808976384 | bytes 1048576 | tf_op jit(solution)/shard_map/sgqb,bk->sgqk/dot_general | solution.py:18
  101.9 7.0 %fusion.13 = f32[2,64,2,512]{3,1,2,0:T(8,128)S(1)} fusion(f32[2,64,2,512]{1,3,2,0:T(8,128)S(1)} %bitcast.116), kind=kOutput, calls=%fused_computation.26 | convolution fusion | flops 808976384 | bytes 1048576 | tf_op jit(solution)/shard_map/sgqb,bk->sgqk/dot_general | solution.py:21
  108.9 7.0 %convolution_add_fusion.1 = f32[2,64,2,512]{3,1,2,0:T(8,128)S(1)} fusion(f32[2,64,2,512]{3,1,2,0:T(8,128)S(1)} %fusion.15, f32[2,64,2,512]{1,3,2,0:T(8,128)S(1)} %bitcast.117), kind=kOutput, calls=%fused_computation.13 | convolution fusion | flops 809107456 | bytes 1572864 | tf_op jit(solution)/shard_map/sgqb,bk->sgqk/dot_general | solution.py:18
  115.9 7.4 %convolution_subtract_fusion.2 = f32[2,64,2,512]{3,1,2,0:T(8,128)S(1)} fusion(f32[2,64,2,512]{3,1,2,0:T(8,128)S(1)} %fusion.13, f32[2,64,2,512]{1,3,2,0:T(8,128)S(1)} %bitcast.115), kind=kOutput, calls=%fused_computation.12 | convolution fusion | flops 809107456 | bytes 1572864 | tf_op jit(solution)/shard_map/sgqb,bk->sgqk/dot_general | solution.py:21
  123.3 4.9 %fusion.9 = f32[2,64,2,512]{3,1,2,0:T(8,128)S(1)} fusion(f32[2,64,2,512]{3,1,2,0:T(8,128)S(1)} %convolution_subtract_fusion.2, f32[2,64,2,512]{3,1,2,0:T(8,128)S(1)} %convolution_add_fusion.1, f32[64,2,512]{2,0,1:T(8,128)S(1)} %copy.39, f32[64,2,512]{2,0,1:T(8,128)S(1)} %copy.36), kind=kOutput, calls=%fused_computation.22 | convolution fusion | flops 809369600 | bytes 2097152 | tf_op jit(solution)/shard_map/sgqk,kb->sgqb/dot_general | solution.py:33
  128.3 4.9 %fusion.11 = f32[2,64,2,512]{3,1,2,0:T(8,128)S(1)} fusion(f32[2,64,2,512]{3,1,2,0:T(8,128)S(1)} %convolution_subtract_fusion.2, f32[2,64,2,512]{3,1,2,0:T(8,128)S(1)} %convolution_add_fusion.1, f32[64,2,512]{2,0,1:T(8,128)S(1)} %copy.39, f32[64,2,512]{2,0,1:T(8,128)S(1)} %copy.36), kind=kOutput, calls=%fused_computation.24 | convolution fusion | flops 809369600 | bytes 2097152 | tf_op jit(solution)/shard_map/sgqk,kb->sgqb/dot_general | solution.py:30
  133.3 5.1 %convolution_add_fusion = f32[2,64,2,512]{3,1,2,0:T(8,128)S(1)} fusion(f32[2,64,2,512]{3,1,2,0:T(8,128)S(1)} %fusion.9, f32[2,64,2,512]{3,1,2,0:T(8,128)S(1)} %convolution_subtract_fusion.2, f32[2,64,2,512]{3,1,2,0:T(8,128)S(1)} %convolution_add_fusion.1, f32[64,2,512]{2,0,1:T(8,128)S(1)} %copy.39, f32[64,2,512]{2,0,1:T(8,128)S(1)} %copy.36), kind=kOutput, calls=%fused_computation.7 | convolution fusion | flops 809500672 | bytes 2621440 | tf_op jit(solution)/shard_map/sgqk,kb->sgqb/dot_general | solution.py:33
  138.4 5.0 %subtract_bitcast_fusion.1 = (f32[1,2,64,2,512]{4,2,3,1,0:T(8,128)S(1)}, f32[1,2,64,2,512]{4,2,3,1,0:T(8,128)S(1)}) fusion(f32[2,64,2,512]{3,1,2,0:T(8,128)S(1)} %convolution_add_fusion, f32[2,512]{1,0:T(2,128)S(1)} %get-tuple-element.16, f32[2,512]{1,0:T(2,128)S(1)} %get-tuple-element.15, f32[2,64,2,512]{3,1,2,0:T(8,128)S(1)} %fusion.11, ...), kind=kOutput, calls=%fused_computation.40 | convolution fusion | flops 810287104 | bytes 3678208 | tf_op jit(solution)/shard_map/sgqk,kb->sgqb/dot_general | solution.py:30
  144.6 3.0 copy.40
  147.5 3.2 reshape.144
  150.7 57.0 %all_to_all.44 = f32[32,1,8192]{2,1,0:T(1,128)S(1)} all-to-all(f32[32,1,8192]{2,1,0:T(1,128)} %reshape.144), channel_id=1, replica_groups=mesh['tensor'=16,'context'=32] {'context'}, dimensions={0} | all-to-all | bytes 2097152 | tf_op jit(solution)/shard_map/all_to_all | solution.py:74
  207.7 4.4 %reduce.1 = f32[32,8192]{1,0:T(8,128)} reduce(f32[32,1,8192]{2,1,0:T(1,128)S(1)} %all_to_all.44, f32[]{:T(128)} %broadcast.231), dimensions={1}, to_apply=%all_to_all.36.reduce_sub_computation | reduce | bytes 2097156 | tf_op jit(solution)/shard_map/all_to_all | solution.py:74
  212.1 2.8 reshape.145
  218.3 48.0 %all_to_all.45 = f32[32,1,2048]{2,1,0:T(1,128)S(1)} all-to-all(f32[32,1,2048]{2,1,0:T(1,128)S(1)} %reshape.146), channel_id=1, replica_groups=mesh['tensor'=16,'context'=32] {'context'}, dimensions={0} | all-to-all | bytes 524288 | tf_op jit(solution)/shard_map/all_to_all | solution.py:80
  266.3 1.3 reduce.2
  268.9 85.8 %all-gather.2.cloned.1.call-done = bf16[2,1024,512]{2,1,0:T(8,128)(2,1)} async-done(((bf16[2,64,512]{2,1,0:T(8,128)(2,1)}), bf16[2,1024,512]{2,1,0:T(8,128)(2,1)}) %all-gather.2.cloned.1.call-update) | async-done | bytes 2097168 | tf_op jit(solution)/shard_map/all_gather | solution.py:104
  354.7 3.1 convolution_convert_fusion
  (43 shorter events, 12.5 us)
Async XLA Ops:
  6.5 348.2 %copy-start = (bf16[1024,256]{1,0:T(8,128)(2,1)S(1)}, bf16[1024,256]{1,0:T(8,128)(2,1)}, u32[]{:S(2)}) copy-start(bf16[1024,256]{1,0:T(8,128)(2,1)} %param.9) | copy-start | bytes 1572868
  8.5 32.6 %all-to-all-start = ((bf16[32,2,1024]{2,1,0:T(2,128)(2,1)}), bf16[32,2,1024]{2,1,0:T(2,128)(2,1)S(1)}, u32[]{:S(2)}, u32[]{:S(2)}) async-start(bf16[32,2,1024]{2,1,0:T(2,128)(2,1)} %reshape.140), calls=%async_computation | async-start | bytes 262144 | tf_op jit(solution)/shard_map/all_to_all | solution.py:46
  44.7 9.3 %copy-start.1 = (f32[2,64,2,512]{3,2,1,0:T(2,128)S(1)}, f32[2,64,2,512]{3,2,1,0:T(2,128)}, u32[]{:S(2)}) copy-start(f32[2,64,2,512]{3,2,1,0:T(2,128)} %param.8) | copy-start | bytes 1572868
  47.0 40.5 %all-to-all-start.1 = ((f32[32,1,8192]{2,1,0:T(1,128)}), f32[32,1,8192]{2,1,0:T(1,128)S(1)}, u32[]{:S(2)}, u32[]{:S(2)}) async-start(f32[32,1,8192]{2,1,0:T(1,128)} %reshape.142), calls=%async_computation.1 | async-start | bytes 2097152 | tf_op jit(solution)/shard_map/all_to_all | solution.py:64
  53.9 300.8 %all-gather.2.cloned.1.call-start = ((), (), s32[]{:S(2)}) async-start(), calls=%async_computation.4 | async-start | bytes 2228224 | tf_op jit(solution)/shard_map/all_gather | solution.py:104
  218.0 50.1 %copy-start.2 = (bf16[2,64,512]{2,1,0:T(8,128)(2,1)S(1)}, bf16[2,64,512]{2,1,0:T(8,128)(2,1)}, u32[]{:S(2)}) copy-start(bf16[2,64,512]{2,1,0:T(8,128)(2,1)} %param.5) | copy-start | bytes 393220
  218.0 50.1 %copy-start.3 = (bf16[2,64,512]{2,1,0:T(8,128)(2,1)S(1)}, bf16[2,64,512]{2,1,0:T(8,128)(2,1)}, u32[]{:S(2)}) copy-start(bf16[2,64,512]{2,1,0:T(8,128)(2,1)} %param.6) | copy-start | bytes 393220
  218.0 50.1 %copy-start.4 = (f32[64]{0:T(128)S(1)}, f32[64]{0:T(128)}, u32[]{:S(2)}) copy-start(f32[64]{0:T(128)} %param.7) | copy-start | bytes 772
Sparse Core Ops, SparseCore 0:
  269.0 85.6 all-gather.1
where the time goes:
time: 372 us; the launch traced here: 365 us
  waiting for transfers between devices  133 us (36%)
  blocking collectives  105 us (28%)
  matrix products  55.4 us (15%)
  starting transfers between devices  25.2 us (7%)
  local copies, waits for them, and re-layouts  19.6 us (5%)
  between operations  14 us (4%)
  other arithmetic  12.5 us (3%)
    all_gather x1, waiting for transfers between devices, local(): lax.all_gather(mixed, 'tensor', axis=1, tiled=True)  85.8 us
    all_to_all x1, blocking collectives, convolve_group(): lax.all_to_all(rotated, 'context', split_axis=4, concat_axis=3, tiled=True)  57 us
    all_to_all x1, blocking collectives, convolve_group(): lax.all_to_all(signal, 'context', split_axis=2, concat_axis=3, tiled=True)  48 us
    all_to_all x1, waiting for transfers between devices, convolve_group(): lax.all_to_all(turned, 'context', split_axis=3, concat_axis=4, tiled=True)  33.2 us
    all_to_all x1, starting transfers between devices, convolve_group(): lax.all_to_all(inputs.reshape(num_seqs, group_ch, peers, slice_len), 'con...  18.2 us
    all_to_all x1, waiting for transfers between devices, convolve_group(): lax.all_to_all(inputs.reshape(num_seqs, group_ch, peers, slice_len), 'con...  14.2 us
    unnamed x19, local copies, waits for them, and re-layouts  13.2 us
  transfers between devices with their start and end apart: 3, of which 3 were waited for; matrix products, arithmetic and copies ran while one was open for 0% of the time, Pallas kernels for 0%

commit v1 on v0

v1 whole, which is shorter than its diff:
```python
import functools
import math

import jax
import jax.numpy as jnp
import ml_dtypes
import numpy as np
from jax import lax
from jax.experimental import pallas as pl
from jax.experimental.pallas import tpu as pltpu
from jax.sharding import PartitionSpec as P

MESH = pl.DeviceIdType.MESH
BF16 = jnp.bfloat16
F32 = jnp.float32

SEQS = 2
PEERS = 32
RING = 4
LOCAL_CH = 64
BLOCK = 512
RES = 64
COLS = 256
FFT = RES * BLOCK


def split_hi_lo(table):
    hi = table.astype(ml_dtypes.bfloat16)
    lo = (table - hi.astype(np.float64)).astype(ml_dtypes.bfloat16)
    return hi, lo


@functools.lru_cache(maxsize=None)
def tables():
    row = np.arange(RES)
    residue = 2 * (row % PEERS) + row // PEERS
    source = np.arange(PEERS)
    pos = np.arange(BLOCK)
    outer = 2.0 * math.pi * (residue[:, None] * source[None, :] % RES) / RES
    first = np.concatenate([np.cos(outer), -np.sin(outer)], axis=0)
    first = np.concatenate(split_hi_lo(first), axis=1)
    last = np.concatenate([np.cos(outer).T, -np.sin(outer).T], axis=1) / FFT
    last_hi, last_lo = split_hi_lo(last)
    last = np.concatenate([last_hi, last_hi, last_lo], axis=1)
    inner = 2.0 * math.pi * (pos[:, None] * pos[None, :] % BLOCK) / BLOCK
    dft = np.stack([*split_hi_lo(np.cos(inner)), *split_hi_lo(np.sin(inner))])
    turn = 2.0 * math.pi * (residue[:, None] * pos[None, :] % FFT) / FFT
    twiddle = np.stack([np.cos(turn), np.sin(turn)]).astype(np.float32)
    return first, last, dft, twiddle


def dot(a, b):
    return jnp.dot(a, b, preferred_element_type=F32)


def split(value):
    hi = value.astype(BF16)
    return hi, (value - hi.astype(F32)).astype(BF16)


def kernel(
    seq_ref, filt_ref, skip_ref, first_ref, last_ref, gate_hbm, w_hbm, dft_hbm, tw_hbm,
    out_ref,
    gate, w_rows, dft, tw, seq32, msg32, sbuf, rbuf, spec, filt32, wide, lhs_hi, lhs_lo,
    bsend, brecv, conv32, skipped, gbuf, wbig, acc,
    load_sem, a2a_sem, z_send, z_recv, y_send, y_recv, h_send, h_recv,
):
    me = lax.axis_index("context")
    t = lax.axis_index("tensor")
    zl, y = t // RING, t % RING
    right = zl * RING + (y + 1) % RING
    left = zl * RING + (y + RING - 1) % RING

    loads = [
        pltpu.make_async_copy(src, dst, load_sem.at[i])
        for i, (src, dst) in enumerate(
            [(dft_hbm, dft), (tw_hbm, tw), (gate_hbm, gate), (w_hbm, w_rows)]
        )
    ]
    for load in loads:
        load.start()

    barrier = pltpu.get_barrier_semaphore()

    def greet(tensor, context):
        pl.semaphore_signal(
            barrier, inc=1, device_id={"tensor": tensor, "context": context}, device_id_type=MESH
        )

    def greet_peer(k, carry):
        greet(t, (me + k) % PEERS)
        return carry

    lax.fori_loop(1, PEERS, greet_peer, 0)
    greet(right, me)
    greet(left, me)

    @pl.when(zl < RING - 1)
    def _():
        greet(t + RING, me)

    @pl.when(zl > 0)
    def _():
        greet(t - RING, me)

    for s in range(SEQS):
        for bh in range(4):
            seq32[bh, pl.ds(s * LOCAL_CH, LOCAL_CH), :] = seq_ref[
                s, :, pl.ds(bh * 128, 128)
            ].astype(F32)
    for s in range(SEQS):
        for chl in range(2):
            for bh in range(4):
                row = (s * 2 + chl) * 4 + bh
                msg32[pl.ds(row, PEERS, stride=16), :] = seq32[
                    bh, pl.ds(s * LOCAL_CH + chl, PEERS, stride=2), :
                ]
    sbuf[:, 0] = msg32[...].reshape(PEERS, 16, 128).astype(BF16)
    parts = filt_ref[...].reshape(2, PEERS, 2, 8, 128)
    for chl in range(2):
        sbuf[:, 1 + chl] = jnp.concatenate([parts[0, :, chl], parts[1, :, chl]], axis=1).astype(BF16)

    z_neighbours = jnp.where(zl < RING - 1, 1, 0) + jnp.where(zl > 0, 1, 0)
    pl.semaphore_wait(barrier, PEERS - 1 + 2 + z_neighbours)

    def exchange(src, dst, first_sem):
        def send(k, carry):
            peer = (me + k) % PEERS
            pltpu.make_async_remote_copy(
                src_ref=src.at[peer],
                dst_ref=dst.at[me],
                send_sem=a2a_sem.at[first_sem],
                recv_sem=a2a_sem.at[first_sem + 1],
                device_id={"tensor": t, "context": peer},
                device_id_type=MESH,
            ).start()
            return carry

        lax.fori_loop(1, PEERS, send, 0)
        dst[me] = src[me]

    def wait_all(buf, sem):
        view = buf.at[pl.ds(0, PEERS - 1)]
        pltpu.make_async_copy(view, view, sem).wait()

    exchange(sbuf, rbuf, 0)

    for load in loads:
        load.wait()
    eye = lax.broadcasted_iota(jnp.int32, (LOCAL_CH, LOCAL_CH), 0) == lax.broadcasted_iota(
        jnp.int32, (LOCAL_CH, LOCAL_CH), 1
    )
    skip_col = jnp.sum(jnp.where(eye, skip_ref[...], 0.0), axis=1, keepdims=True)
    for s in range(SEQS):
        skipped[s] = skip_col * seq_ref[s].astype(F32)
    wbig[...] = jnp.zeros_like(wbig)
    for tt in range(RING * RING):
        rows = w_rows[pl.ds(tt * LOCAL_CH, LOCAL_CH), :]
        wbig[tt, pl.ds(0, LOCAL_CH), pl.ds(0, COLS)] = rows
        wbig[tt, pl.ds(LOCAL_CH, LOCAL_CH), pl.ds(COLS, COLS)] = rows

    wait_all(rbuf, a2a_sem.at[1])
    wait_all(sbuf, a2a_sem.at[0])

    msg32[...] = rbuf[:, 0].reshape(PEERS * 16, 128).astype(F32)
    for s in range(SEQS):
        for chl in range(2):
            row = (s * 2 + chl) * 4
            x = jnp.concatenate(
                [msg32[pl.ds(row + bh, PEERS, stride=16), :] for bh in range(4)], axis=1
            ).astype(BF16)
            freq = dot(first_ref[...], jnp.concatenate([x, x], axis=0))
            re, im = freq[:RES], freq[RES:]
            base = (s * 2 + chl) * RES
            for part, value in enumerate((re * tw[0] + im * tw[1], im * tw[0] - re * tw[1])):
                hi, lo = split(value)
                lhs_hi[pl.ds(part * 4 * RES + base, RES), :] = hi
                lhs_lo[pl.ds(part * 4 * RES + base, RES), :] = lo
    for chl in range(2):
        filt32[...] = rbuf[:, 1 + chl].reshape(PEERS * 16, 128).astype(F32)
        for ri in range(2):
            for j in range(2):
                for mh in range(4):
                    spec[ri, pl.ds(chl * RES + j * PEERS, PEERS), pl.ds(mh * 128, 128)] = filt32[
                        pl.ds(ri * 8 + mh * 2 + j, PEERS, stride=16), :
                    ]

    def inner(which):
        hi, lo = lhs_hi[...], lhs_lo[...]
        return dot(hi, dft[2 * which]) + dot(lo, dft[2 * which]) + dot(hi, dft[2 * which + 1])

    half = 4 * RES
    wide[0] = inner(0)
    wide[1] = inner(1)
    for s in range(SEQS):
        rows = pl.ds(s * 2 * RES, 2 * RES)
        rows_im = pl.ds(half + s * 2 * RES, 2 * RES)
        f_re = wide[0, rows, :] + wide[1, rows_im, :]
        f_im = wide[0, rows_im, :] - wide[1, rows, :]
        for which, value in (
            (rows, f_re * spec[0] - f_im * spec[1]),
            (rows_im, f_re * spec[1] + f_im * spec[0]),
        ):
            hi, lo = split(value)
            lhs_hi[which, :] = hi
            lhs_lo[which, :] = lo
    wide[0] = inner(0)
    wide[1] = inner(1)
    for s in range(SEQS):
        for chl in range(2):
            base = (s * 2 + chl) * RES
            rows, rows_im = pl.ds(base, RES), pl.ds(half + base, RES)
            b_re = wide[0, rows, :] - wide[1, rows_im, :]
            b_im = wide[0, rows_im, :] + wide[1, rows, :]
            re_hi, re_lo = split(b_re * tw[0] - b_im * tw[1])
            im_hi, im_lo = split(b_im * tw[0] + b_re * tw[1])
            signal = dot(
                last_ref[...],
                jnp.concatenate([re_hi, im_hi, re_lo, im_lo, re_hi, im_hi], axis=0),
            )
            for bh in range(4):
                msg32[pl.ds((s * 2 + chl) * 4 + bh, PEERS, stride=16), :] = signal[
                    :, bh * 128 : (bh + 1) * 128
                ]
    bsend[...] = msg32[...].reshape(PEERS, 16, 128).astype(BF16)

    exchange(bsend, brecv, 2)
    wait_all(brecv, a2a_sem.at[3])
    wait_all(bsend, a2a_sem.at[2])

    msg32[...] = brecv[...].reshape(PEERS * 16, 128).astype(F32)
    for s in range(SEQS):
        for chl in range(2):
            for bh in range(4):
                row = (s * 2 + chl) * 4 + bh
                conv32[bh, pl.ds(s * LOCAL_CH + chl, PEERS, stride=2), :] = msg32[
                    pl.ds(row, PEERS, stride=16), :
                ]
    for bh in range(4):
        lanes = pl.ds(bh * 128, 128)
        mixed = jnp.concatenate(
            [
                gate[s, :, lanes].astype(F32)
                * (conv32[bh, pl.ds(s * LOCAL_CH, LOCAL_CH), :] + skipped[s, :, lanes])
                for s in range(SEQS)
            ],
            axis=0,
        )
        gbuf[t, lanes, :] = mixed.T.astype(BF16)

    def copy(slot, rows, send_sem, recv_sem, target):
        ref = gbuf.at[slot, rows]
        return pltpu.make_async_remote_copy(
            src_ref=ref,
            dst_ref=ref,
            send_sem=send_sem,
            recv_sem=recv_sem,
            device_id={"tensor": target, "context": me},
            device_id_type=MESH,
        )

    whole, front, back = pl.ds(0, BLOCK), pl.ds(0, BLOCK // 2), pl.ds(BLOCK // 2, BLOCK // 2)

    def up(k):
        return copy(t - k * RING, whole, z_send.at[0, k], z_recv.at[0, k], t + RING)

    def down(k):
        return copy(t + k * RING, whole, z_send.at[1, k], z_recv.at[1, k], t - RING)

    def y_copies(z):
        slot = z * RING + y
        return (
            copy(slot, whole, y_send.at[0, z], y_recv.at[0, z], right),
            copy(slot, whole, y_send.at[1, z], y_recv.at[1, z], left),
        )

    def y_halves(z):
        return (
            copy(z * RING + (y + RING - 1) % RING, front, h_send.at[0, z], h_recv.at[0, z], right),
            copy(z * RING + (y + 1) % RING, back, h_send.at[1, z], h_recv.at[1, z], left),
        )

    def opposite(z):
        slot = z * RING + (y + 2) % RING
        return (
            copy(slot, front, h_send.at[0, z], h_recv.at[0, z], right),
            copy(slot, back, h_send.at[1, z], h_recv.at[1, z], left),
        )

    def forward_y(z):
        for arrived, half_copy in zip(
            (
                copy(z * RING + (y + RING - 1) % RING, whole, y_send.at[0, z], y_recv.at[0, z], right),
                copy(z * RING + (y + 1) % RING, whole, y_send.at[1, z], y_recv.at[1, z], left),
            ),
            y_halves(z),
        ):
            arrived.wait_recv()
            half_copy.start()

    @pl.when(zl < RING - 1)
    def _():
        up(0).start()

    @pl.when(zl > 0)
    def _():
        down(0).start()

    for c in y_copies(zl):
        c.start()

    for k in range(1, RING):

        @pl.when(zl >= k)
        def _():
            copy(t - k * RING, whole, z_send.at[0, k - 1], z_recv.at[0, k - 1], t).wait_recv()

            @pl.when(zl < RING - 1)
            def _():
                up(k).start()

            for c in y_copies(zl - k):
                c.start()

        @pl.when(zl < RING - k)
        def _():
            copy(t + k * RING, whole, z_send.at[1, k - 1], z_recv.at[1, k - 1], t).wait_recv()

            @pl.when(zl > 0)
            def _():
                down(k).start()

            for c in y_copies(zl + k):
                c.start()

        if k == 1:
            forward_y(zl)
        else:

            @pl.when(zl >= k - 1)
            def _():
                forward_y(zl - (k - 1))

            @pl.when(zl < RING - (k - 1))
            def _():
                forward_y(zl + (k - 1))

    @pl.when(zl >= RING - 1)
    def _():
        forward_y(zl - (RING - 1))

    @pl.when(zl < 1)
    def _():
        forward_y(zl + (RING - 1))

    def project(column):
        total = None
        for zp in range(0, RING, 2):
            ta, tb = zp * RING + column, (zp + 1) * RING + column
            term = dot(
                jnp.concatenate([gbuf[ta], gbuf[tb]], axis=1),
                jnp.concatenate([wbig[ta], wbig[tb]], axis=0),
            )
            total = term if total is None else total + term
        return total

    acc[...] = project(y)
    acc[...] += project((y + RING - 1) % RING)
    acc[...] += project((y + 1) % RING)
    for z in range(RING):
        for c in opposite(z):
            c.wait_recv()
    total = acc[...] + project((y + 2) % RING)
    for s in range(SEQS):
        out_ref[s] = total[:, s * COLS : (s + 1) * COLS].astype(BF16)

    for k in range(RING - 1):

        @pl.when((zl >= k) & (zl < RING - 1))
        def _():
            up(k).wait_send()

        @pl.when((zl < RING - k) & (zl > 0))
        def _():
            down(k).wait_send()

    for z in range(RING):
        for c in y_copies(z):
            c.wait_send()
        for c in y_halves(z):
            c.wait_send()


def local(sequence, gate, skip, filter_spectrum, out_weight):
    first, last, dft, twiddle = tables()
    rows = filter_spectrum.reshape(2, LOCAL_CH, 2, 4, 128).transpose(0, 1, 3, 2, 4).reshape(-1, 128)
    vmem = pl.BlockSpec(memory_space=pltpu.VMEM)
    hbm = pl.BlockSpec(memory_space=pl.ANY)
    return pl.pallas_call(
        kernel,
        out_shape=jax.ShapeDtypeStruct((SEQS, BLOCK, COLS), BF16),
        in_specs=[vmem] * 5 + [hbm] * 4,
        out_specs=vmem,
        scratch_shapes=[
            pltpu.VMEM((SEQS, LOCAL_CH, BLOCK), BF16),
            pltpu.VMEM((RING * RING * LOCAL_CH, COLS), BF16),
            pltpu.VMEM((4, BLOCK, BLOCK), BF16),
            pltpu.VMEM((2, RES, BLOCK), F32),
            pltpu.VMEM((4, SEQS * LOCAL_CH, 128), F32),
            pltpu.VMEM((PEERS * 16, 128), F32),
            pltpu.VMEM((PEERS, 3, 16, 128), BF16),
            pltpu.VMEM((PEERS, 3, 16, 128), BF16),
            pltpu.VMEM((2, 2 * RES, BLOCK), F32),
            pltpu.VMEM((PEERS * 16, 128), F32),
            pltpu.VMEM((2, 8 * RES, BLOCK), F32),
            pltpu.VMEM((8 * RES, BLOCK), BF16),
            pltpu.VMEM((8 * RES, BLOCK), BF16),
            pltpu.VMEM((PEERS, 16, 128), BF16),
            pltpu.VMEM((PEERS, 16, 128), BF16),
            pltpu.VMEM((4, SEQS * LOCAL_CH, 128), F32),
            pltpu.VMEM((SEQS, LOCAL_CH, BLOCK), F32),
            pltpu.VMEM((RING * RING, BLOCK, 128), BF16),
            pltpu.VMEM((RING * RING, 128, 2 * COLS), BF16),
            pltpu.VMEM((BLOCK, 2 * COLS), F32),
            pltpu.SemaphoreType.DMA((4,)),
            pltpu.SemaphoreType.DMA((4,)),
            pltpu.SemaphoreType.DMA((2, RING)),
            pltpu.SemaphoreType.DMA((2, RING)),
            pltpu.SemaphoreType.DMA((2, RING)),
            pltpu.SemaphoreType.DMA((2, RING)),
            pltpu.SemaphoreType.DMA((2, RING)),
            pltpu.SemaphoreType.DMA((2, RING)),
        ],
        compiler_params=pltpu.CompilerParams(
            collective_id=0, has_side_effects=True, vmem_limit_bytes=48 * 1024 * 1024
        ),
    )(
        sequence, rows, skip.reshape(1, LOCAL_CH), jnp.asarray(first), jnp.asarray(last),
        gate, out_weight, jnp.asarray(dft), jnp.asarray(twiddle),
    )


def solution(mesh):
    in_specs = (
        P(None, "tensor", "context"),
        P(None, "tensor", "context"),
        P("tensor"),
        P(None, "tensor", "context", None),
        P(None, "tensor"),
    )
    out_specs = P(None, "context", "tensor")
    return jax.shard_map(local, mesh=mesh, in_specs=in_specs, out_specs=out_specs, check_vma=False)
```

time: 372 us -> 89.9 us (0.24); the launches traced: 365 us -> 89.4 us
  waiting for transfers between devices: 133 us -> 0 us
  blocking collectives: 105 us -> 0 us
  Pallas kernels: 0 us -> 80 us
  matrix products: 55.4 us -> 0 us
  starting transfers between devices: 25.2 us -> 0 us
  between operations: 14 us -> 0.02 us
  other arithmetic: 12.5 us -> 0 us
  local copies, waits for them, and re-layouts: 19.6 us -> 9.37 us
    all_to_all x2 -> x0, blocking collectives: 105 us -> none  [the longest x1 57 us: convolve_group(): lax.all_to_all(rotated, 'context', split_axis=4, concat_axis=3, tiled=True)]
    all_gather x1 -> x0, waiting for transfers between devices: 85.8 us -> none  [local(): lax.all_gather(mixed, 'tensor', axis=1, tiled=True)]
    pallas_call x0 -> x1, Pallas kernels: none -> 80 us  [local(): pl.pallas_call(kernel, out_shape=jax.ShapeDtypeStruct((SEQS, BLOCK, COLS)...]
    dot_general x13 -> x0, matrix products: 55.4 us -> none  [the longest x1 7.42 us: inner_forward(): jnp.einsum('sgqb,bk->sgqk', col_re, sin_b, precision=precise)]
    all_to_all x2 -> x0, waiting for transfers between devices: 47.4 us -> none  [the longest x1 33.2 us: convolve_group(): lax.all_to_all(turned, 'context', split_axis=3, concat_axis=4, tiled=True)]
    all_to_all x2 -> x0, starting transfers between devices: 25.2 us -> none  [the longest x1 18.2 us: convolve_group(): lax.all_to_all(inputs.reshape(num_seqs, group_ch, peers, slice_len), 'con...]
    all_to_all x3 -> x0, other arithmetic: 10.1 us -> none  [the longest x1 4.42 us: convolve_group(): lax.all_to_all(rotated, 'context', split_axis=4, concat_axis=3, tiled=True)]
    another operation x2 -> x0, local copies, waits for them, and re-layouts: 4.18 us -> none  [the longest x1 2.97 us: convolve_group(): jnp.stack([back_re * cos_i - back_im * sin_i, back_im * cos_i + back_re *...]
  transfers between devices with their start and end apart: 3 -> 0, of which waited for: 3 -> 0; matrix products, arithmetic and copies ran while one was open for 0% -> 0% of each run, Pallas kernels for 0% -> 0%
where the time goes in v1:
time: 89.9 us; the launch traced here: 89.4 us
  Pallas kernels  80 us (89%)
  local copies, waits for them, and re-layouts  9.37 us (10%)
    pallas_call x1, Pallas kernels, local(): pl.pallas_call(kernel, out_shape=jax.ShapeDtypeStruct((SEQS, BLOCK, COLS)...  80 us
    unnamed x19, local copies, waits for them, and re-layouts  9.37 us

profile of v1, /device:TPU:2, one launch (start us, length us, event | category | flops | bytes accessed | tf_op | source)
XLA Modules:
  0.0 89.4 jit_solution(2861083521172158515)
XLA Ops:
  0.0 0.0 copy-start
  0.0 1.6 %copy-done = bf16[4,512,512]{2,1,0:T(8,128)(2,1)S(1)} copy-done((bf16[4,512,512]{2,1,0:T(8,128)(2,1)S(1)}, bf16[4,512,512]{2,1,0:T(8,128)(2,1)}, u32[]{:S(2)}) %copy-start) | copy-done | bytes 2097176
  1.6 0.0 copy-start.1
  1.6 1.0 %copy-done.1 = f32[2,64,2,512]{3,2,1,0:T(2,128)S(1)} copy-done((f32[2,64,2,512]{3,2,1,0:T(2,128)S(1)}, f32[2,64,2,512]{3,2,1,0:T(2,128)}, u32[]{:S(2)}) %copy-start.1) | copy-done | bytes 524312
  2.6 0.0 copy-start.2
  2.6 1.0 %copy-done.2 = bf16[1024,256]{1,0:T(8,128)(2,1)S(1)} copy-done((bf16[1024,256]{1,0:T(8,128)(2,1)S(1)}, bf16[1024,256]{1,0:T(8,128)(2,1)}, u32[]{:S(2)}) %copy-start.2) | copy-done | bytes 524312
  3.7 0.0 copy-start.3
  3.7 0.9 %copy-done.3 = f32[2,64,512]{2,1,0:T(8,128)S(1)} copy-done((f32[2,64,512]{2,1,0:T(8,128)S(1)}, f32[2,64,512]{2,1,0:T(8,128)}, u32[]{:S(2)}) %copy-start.3) | copy-done | bytes 262168
  4.6 0.0 copy-start.4
  4.6 0.9 %copy-done.4 = bf16[2,64,512]{2,1,0:T(8,128)(2,1)S(1)} copy-done((bf16[2,64,512]{2,1,0:T(8,128)(2,1)S(1)}, bf16[2,64,512]{2,1,0:T(8,128)(2,1)}, u32[]{:S(2)}) %copy-start.4) | copy-done | bytes 131096
  5.5 0.0 copy-start.5
  5.5 0.9 %copy-done.5 = bf16[2,64,512]{2,1,0:T(8,128)(2,1)S(1)} copy-done((bf16[2,64,512]{2,1,0:T(8,128)(2,1)S(1)}, bf16[2,64,512]{2,1,0:T(8,128)(2,1)}, u32[]{:S(2)}) %copy-start.5) | copy-done | bytes 131096
  6.4 0.0 copy-start.6
  6.4 0.8 copy-done.6
  7.2 0.0 copy-start.7
  7.2 0.7 copy-done.7
  7.9 0.0 copy-start.8
  7.9 0.7 copy-done.8
  8.6 80.0 %shard_map.91 = bf16[2,512,256]{2,1,0:T(8,128)(2,1)S(1)} custom-call(bf16[2,64,512]{2,1,0:T(8,128)(2,1)S(1)} %copy-done.4, f32[1024,128]{1,0:T(8,128)S(1)} %bitcast.6, f32[1,64]{1,0:T(1,128)S(1)} %bitcast.7, bf16[128,64]{1,0:T(8,128)(2,1)S(1)} %copy-done.6, bf16[32,384]{1,0:T(8,128)(2,1)S(1)} %copy-done.7, bf16[2,64,512]{2,1,0:T(8,128)(2,1)S(1)} %copy-done.5, ...), custom_call_target="tpu_custom_call" | custom-call | tf_op jit(solution)/shard_map/pallas_call | solution.py:399
  88.6 0.8 copy.12
Async XLA Ops:
  0.0 1.6 %copy-start = (bf16[4,512,512]{2,1,0:T(8,128)(2,1)S(1)}, bf16[4,512,512]{2,1,0:T(8,128)(2,1)}, u32[]{:S(2)}) copy-start(bf16[4,512,512]{2,1,0:T(8,128)(2,1)} %constant.10.clone.dft_hbm) | copy-start | bytes 6291460
  1.6 1.0 %copy-start.1 = (f32[2,64,2,512]{3,2,1,0:T(2,128)S(1)}, f32[2,64,2,512]{3,2,1,0:T(2,128)}, u32[]{:S(2)}) copy-start(f32[2,64,2,512]{3,2,1,0:T(2,128)} %param.12) | copy-start | bytes 1572868
  2.6 1.0 %copy-start.2 = (bf16[1024,256]{1,0:T(8,128)(2,1)S(1)}, bf16[1024,256]{1,0:T(8,128)(2,1)}, u32[]{:S(2)}) copy-start(bf16[1024,256]{1,0:T(8,128)(2,1)} %w_hbm.1) | copy-start | bytes 1572868
  3.7 0.9 %copy-start.3 = (f32[2,64,512]{2,1,0:T(8,128)S(1)}, f32[2,64,512]{2,1,0:T(8,128)}, u32[]{:S(2)}) copy-start(f32[2,64,512]{2,1,0:T(8,128)} %constant.11.clone.tw_hbm) | copy-start | bytes 786436
  4.6 0.9 %copy-start.4 = (bf16[2,64,512]{2,1,0:T(8,128)(2,1)S(1)}, bf16[2,64,512]{2,1,0:T(8,128)(2,1)}, u32[]{:S(2)}) copy-start(bf16[2,64,512]{2,1,0:T(8,128)(2,1)} %seq_ref.1) | copy-start | bytes 393220
  5.5 0.9 %copy-start.5 = (bf16[2,64,512]{2,1,0:T(8,128)(2,1)S(1)}, bf16[2,64,512]{2,1,0:T(8,128)(2,1)}, u32[]{:S(2)}) copy-start(bf16[2,64,512]{2,1,0:T(8,128)(2,1)} %gate_hbm.1) | copy-start | bytes 393220
  6.4 0.8 copy-start.6
  7.2 0.7 copy-start.7
  7.9 0.7 copy-start.8

commit v2 on v1

v2 whole, which is shorter than its diff:
```python
import functools
import math

import jax
import jax.numpy as jnp
import ml_dtypes
import numpy as np
from jax import lax
from jax.experimental import pallas as pl
from jax.experimental.pallas import tpu as pltpu
from jax.sharding import PartitionSpec as P

MESH = pl.DeviceIdType.MESH
BF16 = jnp.bfloat16
F32 = jnp.float32

SEQS = 2
PEERS = 32
RING = 4
LOCAL_CH = 64
BLOCK = 512
RES = 64
COLS = 256
FFT = RES * BLOCK


def split_hi_lo(table):
    hi = table.astype(ml_dtypes.bfloat16)
    lo = (table - hi.astype(np.float64)).astype(ml_dtypes.bfloat16)
    return hi, lo


@functools.lru_cache(maxsize=None)
def tables():
    row = np.arange(RES)
    residue = 2 * (row % PEERS) + row // PEERS
    source = np.arange(PEERS)
    pos = np.arange(BLOCK)
    outer = 2.0 * math.pi * (residue[:, None] * source[None, :] % RES) / RES
    first = np.concatenate([np.cos(outer), -np.sin(outer)], axis=0)
    first = np.concatenate(split_hi_lo(first), axis=1)
    last = np.concatenate([np.cos(outer).T, -np.sin(outer).T], axis=1) / FFT
    last_hi, last_lo = split_hi_lo(last)
    last = np.concatenate([last_hi, last_hi, last_lo], axis=1)
    inner = 2.0 * math.pi * (pos[:, None] * pos[None, :] % BLOCK) / BLOCK
    dft = np.stack([*split_hi_lo(np.cos(inner)), *split_hi_lo(np.sin(inner))])
    turn = 2.0 * math.pi * (residue[:, None] * pos[None, :] % FFT) / FFT
    twiddle = np.stack([np.cos(turn), np.sin(turn)]).astype(np.float32)
    return first, last, dft, twiddle


def dot(a, b):
    return jnp.dot(a, b, preferred_element_type=F32)


def split(value):
    hi = value.astype(BF16)
    return hi, (value - hi.astype(F32)).astype(BF16)


def kernel(
    seq_hbm, filt_hbm, skip_hbm, first_hbm, last_hbm, gate_hbm, w_hbm, dft_hbm, tw_hbm,
    out_ref,
    seq, filt, skip, first, last, gate, w_rows, dft, tw,
    seq32, gate32, skipped, w32, msg32, sseq, rseq, sfilt, rfilt, spec, wide, lhs_hi, lhs_lo,
    bsend, brecv, gbuf, wrep, acc,
    load_sem, a2a_send, a2a_recv, z_send, z_recv, y_send, y_recv, h_send, h_recv,
):
    me = lax.axis_index("context")
    t = lax.axis_index("tensor")
    x, zh, core = me // 8, (me // 2) % 4, me % 2
    zl, y = t // RING, t % RING
    right = zl * RING + (y + 1) % RING
    left = zl * RING + (y + RING - 1) % RING

    def over_peers(visit):
        def step(j, carry):
            visit(
                ((x + 2 + (j // 2) % 4) % 4) * 8 + ((zh + 2 + j // 8) % 4) * 2 + (core + j) % 2
            )
            return carry

        lax.fori_loop(0, 20, step, 0)
        lax.fori_loop(21, PEERS, step, 0)

    barrier = pltpu.get_barrier_semaphore()

    def greet(tensor, context):
        pl.semaphore_signal(
            barrier, inc=1, device_id={"tensor": tensor, "context": context}, device_id_type=MESH
        )

    over_peers(lambda peer: greet(t, peer))
    greet(right, me)
    greet(left, me)

    @pl.when(zl < RING - 1)
    def _():
        greet(t + RING, me)

    @pl.when(zl > 0)
    def _():
        greet(t - RING, me)

    loads = [
        pltpu.make_async_copy(src, dst, load_sem.at[i])
        for i, (src, dst) in enumerate(
            [
                (seq_hbm, seq), (filt_hbm, filt), (skip_hbm, skip), (first_hbm, first),
                (last_hbm, last), (gate_hbm, gate), (w_hbm, w_rows), (tw_hbm, tw), (dft_hbm, dft),
            ]
        )
    ]
    for load in loads:
        load.start()

    loads[0].wait()
    for s in range(SEQS):
        for bh in range(4):
            seq32[bh, pl.ds(s * LOCAL_CH, LOCAL_CH), :] = seq[s, :, pl.ds(bh * 128, 128)].astype(F32)
    for s in range(SEQS):
        for chl in range(2):
            for bh in range(4):
                msg32[pl.ds((s * 2 + chl) * 4 + bh, PEERS, stride=16), :] = seq32[
                    bh, pl.ds(s * LOCAL_CH + chl, PEERS, stride=2), :
                ]
    sseq[...] = msg32[...].reshape(PEERS, 16, 128).astype(BF16)
    loads[1].wait()
    parts = filt[...].reshape(2, PEERS, 2, 8, 128)
    for chl in range(2):
        sfilt[chl] = jnp.concatenate([parts[0, :, chl], parts[1, :, chl]], axis=1).astype(BF16)

    z_neighbours = jnp.where(zl < RING - 1, 1, 0) + jnp.where(zl > 0, 1, 0)
    pl.semaphore_wait(barrier, PEERS - 1 + 2 + z_neighbours)

    def exchange(src, dst, sem):
        def send(peer):
            pltpu.make_async_remote_copy(
                src_ref=src.at[peer],
                dst_ref=dst.at[me],
                send_sem=a2a_send.at[sem],
                recv_sem=a2a_recv.at[sem],
                device_id={"tensor": t, "context": peer},
                device_id_type=MESH,
            ).start()

        over_peers(send)
        dst[me] = src[me]

    def wait_all(buf, sem):
        view = buf.at[pl.ds(0, PEERS - 1)]
        pltpu.make_async_copy(view, view, sem).wait()

    exchange(sseq, rseq, 0)
    exchange(sfilt.at[0], rfilt.at[0], 1)
    exchange(sfilt.at[1], rfilt.at[1], 2)

    for load in loads[2:]:
        load.wait()
    eye = lax.broadcasted_iota(jnp.int32, (LOCAL_CH, LOCAL_CH), 0) == lax.broadcasted_iota(
        jnp.int32, (LOCAL_CH, LOCAL_CH), 1
    )
    skip_col = jnp.sum(jnp.where(eye, skip[...], 0.0), axis=1, keepdims=True)
    for s in range(SEQS):
        rows = pl.ds(s * LOCAL_CH, LOCAL_CH)
        for bh in range(4):
            skipped[bh, rows, :] = skip_col * seq32[bh, rows, :]
            gate32[bh, rows, :] = gate[s, :, pl.ds(bh * 128, 128)].astype(F32)
    for half in range(2):
        lanes = pl.ds(half * 128, 128)
        w32[half] = w_rows[:, lanes].astype(F32)
        for tt in range(RING * RING):
            for chl in range(2):
                rows = w32[half, pl.ds(tt * LOCAL_CH + chl, PEERS, stride=2), :].astype(BF16)
                for copy_of in range(4):
                    wrep[tt, pl.ds(chl * 128 + copy_of * PEERS, PEERS), lanes] = rows

    wait_all(rseq, a2a_recv.at[0])
    msg32[...] = rseq[...].reshape(PEERS * 16, 128).astype(F32)

    def base(chl, part, s):
        return ((chl * 2 + part) * 2 + s) * RES

    for chl in range(2):
        for s in range(SEQS):
            row = (s * 2 + chl) * 4
            tokens = jnp.concatenate(
                [msg32[pl.ds(row + bh, PEERS, stride=16), :] for bh in range(4)], axis=1
            ).astype(BF16)
            freq = dot(first[...], jnp.concatenate([tokens, tokens], axis=0))
            re, im = freq[:RES], freq[RES:]
            for part, value in enumerate((re * tw[0] + im * tw[1], im * tw[0] - re * tw[1])):
                hi, lo = split(value)
                lhs_hi[pl.ds(base(chl, part, s), RES), :] = hi
                lhs_lo[pl.ds(base(chl, part, s), RES), :] = lo

    def inner(which, rows):
        hi, lo = lhs_hi[rows, :], lhs_lo[rows, :]
        return dot(hi, dft[2 * which]) + dot(lo, dft[2 * which]) + dot(hi, dft[2 * which + 1])

    everything = pl.ds(0, 8 * RES)
    wide[0] = inner(0, everything)
    wide[1] = inner(1, everything)

    for chl in range(2):
        wait_all(rfilt.at[chl], a2a_recv.at[1 + chl])
        msg32[...] = rfilt[chl].reshape(PEERS * 16, 128).astype(F32)
        for ri in range(2):
            for j in range(2):
                for mh in range(4):
                    spec[ri, pl.ds(j * PEERS, PEERS), pl.ds(mh * 128, 128)] = msg32[
                        pl.ds(ri * 8 + mh * 2 + j, PEERS, stride=16), :
                    ]
        for s in range(SEQS):
            rows, rows_im = pl.ds(base(chl, 0, s), RES), pl.ds(base(chl, 1, s), RES)
            f_re = wide[0, rows, :] + wide[1, rows_im, :]
            f_im = wide[0, rows_im, :] - wide[1, rows, :]
            for which, value in (
                (rows, f_re * spec[0] - f_im * spec[1]),
                (rows_im, f_re * spec[1] + f_im * spec[0]),
            ):
                hi, lo = split(value)
                lhs_hi[which, :] = hi
                lhs_lo[which, :] = lo
        channel = pl.ds(chl * 4 * RES, 4 * RES)
        wide[0, channel, :] = inner(0, channel)
        wide[1, channel, :] = inner(1, channel)
        for s in range(SEQS):
            rows, rows_im = pl.ds(base(chl, 0, s), RES), pl.ds(base(chl, 1, s), RES)
            b_re = wide[0, rows, :] - wide[1, rows_im, :]
            b_im = wide[0, rows_im, :] + wide[1, rows, :]
            re_hi, re_lo = split(b_re * tw[0] - b_im * tw[1])
            im_hi, im_lo = split(b_im * tw[0] + b_re * tw[1])
            signal = dot(
                last[...], jnp.concatenate([re_hi, im_hi, re_lo, im_lo, re_hi, im_hi], axis=0)
            )
            for bh in range(4):
                msg32[pl.ds(s * 4 + bh, PEERS, stride=8), :] = signal[:, bh * 128 : (bh + 1) * 128]
        bsend[chl] = msg32[pl.ds(0, PEERS * 8), :].reshape(PEERS, 8, 128).astype(BF16)
        exchange(bsend.at[chl], brecv.at[chl], 3 + chl)

    def mix(chl):
        wait_all(brecv.at[chl], a2a_recv.at[3 + chl])
        msg32[pl.ds(0, PEERS * 8), :] = brecv[chl].astype(F32).reshape(PEERS * 8, 128)
        for block in range(2):
            pieces = []
            for half in range(2):
                bh = half * 2 + block
                for s in range(SEQS):
                    rows = pl.ds(s * LOCAL_CH + chl, PEERS, stride=2)
                    conv = msg32[pl.ds(s * 4 + bh, PEERS, stride=8), :]
                    pieces.append(gate32[bh, rows, :] * (conv + skipped[bh, rows, :]))
            mixed = jnp.concatenate(pieces, axis=0)
            gbuf[t, chl, pl.ds(block * 128, 128), :] = mixed.T.astype(BF16)

    def copy(slot, chl, rows, send_sem, recv_sem, target):
        ref = gbuf.at[slot, chl, rows]
        return pltpu.make_async_remote_copy(
            src_ref=ref,
            dst_ref=ref,
            send_sem=send_sem,
            recv_sem=recv_sem,
            device_id={"tensor": target, "context": me},
            device_id_type=MESH,
        )

    whole, front, back = pl.ds(0, 256), pl.ds(0, 128), pl.ds(128, 128)
    beyond_left, beyond_right = (y + RING - 1) % RING, (y + 1) % RING

    def up(k, chl):
        return copy(t - k * RING, chl, whole, z_send.at[0, k, chl], z_recv.at[0, k, chl], t + RING)

    def down(k, chl):
        return copy(t + k * RING, chl, whole, z_send.at[1, k, chl], z_recv.at[1, k, chl], t - RING)

    def y_copies(z, chl, column_right=None, column_left=None):
        return (
            copy(z * RING + (y if column_right is None else column_right), chl, whole,
                 y_send.at[0, z, chl], y_recv.at[0, z, chl], right),
            copy(z * RING + (y if column_left is None else column_left), chl, whole,
                 y_send.at[1, z, chl], y_recv.at[1, z, chl], left),
        )

    def y_halves(z, chl, column_right, column_left):
        return (
            copy(z * RING + column_right, chl, front, h_send.at[0, z, chl], h_recv.at[0, z, chl], right),
            copy(z * RING + column_left, chl, back, h_send.at[1, z, chl], h_recv.at[1, z, chl], left),
        )

    def start_own(chl):
        @pl.when(zl < RING - 1)
        def _():
            up(0, chl).start()

        @pl.when(zl > 0)
        def _():
            down(0, chl).start()

        for c in y_copies(zl, chl):
            c.start()

    def on_levels(k, visit):
        if k == 0:
            visit(zl)
            return

        @pl.when(zl >= k)
        def _():
            visit(zl - k)

        @pl.when(zl < RING - k)
        def _():
            visit(zl + k)

    def z_step(k, chl):
        @pl.when(zl >= k)
        def _():
            copy(t - k * RING, chl, whole, z_send.at[0, k - 1, chl], z_recv.at[0, k - 1, chl], t).wait_recv()

            @pl.when(zl < RING - 1)
            def _():
                up(k, chl).start()

            for c in y_copies(zl - k, chl):
                c.start()

        @pl.when(zl < RING - k)
        def _():
            copy(t + k * RING, chl, whole, z_send.at[1, k - 1, chl], z_recv.at[1, k - 1, chl], t).wait_recv()

            @pl.when(zl > 0)
            def _():
                down(k, chl).start()

            for c in y_copies(zl + k, chl):
                c.start()

    def y_step(k, chl):
        def visit(z):
            for arrived, half in zip(
                y_copies(z, chl, beyond_left, beyond_right), y_halves(z, chl, beyond_left, beyond_right)
            ):
                arrived.wait_recv()
                half.start()

        on_levels(k, visit)

    lane_group = lax.broadcasted_iota(jnp.int32, (256, 2 * 128), 1) % 128 // PEERS

    def project(slot):
        both = jnp.concatenate([gbuf[slot, 0], gbuf[slot, 1]], axis=1)
        stacked = jnp.concatenate(
            [jnp.where(lane_group == group, both, jnp.zeros_like(both)) for group in range(4)], axis=0
        )
        acc[...] += dot(stacked, wrep[slot])

    def project_near(k):
        def visit(z):
            for column in (y, beyond_left, beyond_right):
                project(z * RING + column)

        on_levels(k, visit)

    def project_far(k):
        def visit(z):
            column = (y + 2) % RING
            for chl in range(2):
                for c in y_halves(z, chl, column, column):
                    c.wait_recv()
            project(z * RING + column)

        on_levels(k, visit)

    acc[...] = jnp.zeros_like(acc)
    mix(0)
    start_own(0)
    z_step(1, 0)
    y_step(0, 0)
    mix(1)
    start_own(1)
    z_step(2, 0)
    y_step(1, 0)
    z_step(1, 1)
    y_step(0, 1)
    z_step(3, 0)
    y_step(2, 0)
    z_step(2, 1)
    y_step(1, 1)
    project_near(0)
    z_step(3, 1)
    y_step(3, 0)
    y_step(2, 1)
    project_near(1)
    y_step(3, 1)
    project_far(0)
    project_near(2)
    project_far(1)
    project_near(3)
    project_far(2)
    project_far(3)

    for group in range(4):
        out_ref[group % 2, pl.ds(group // 2 * 256, 256), :] = acc[pl.ds(group * 256, 256), :].astype(BF16)

    for i, buf in enumerate((sseq, sfilt.at[0], sfilt.at[1], bsend.at[0], bsend.at[1])):
        wait_all(buf, a2a_send.at[i])
    for chl in range(2):
        for k in range(RING - 1):

            @pl.when((zl >= k) & (zl < RING - 1))
            def _():
                up(k, chl).wait_send()

            @pl.when((zl < RING - k) & (zl > 0))
            def _():
                down(k, chl).wait_send()

        for z in range(RING):
            for c in y_copies(z, chl) + y_halves(z, chl, y, y):
                c.wait_send()


def local(sequence, gate, skip, filter_spectrum, out_weight):
    first, last, dft, twiddle = tables()
    rows = filter_spectrum.reshape(2, LOCAL_CH, 2, 4, 128).transpose(0, 1, 3, 2, 4).reshape(-1, 128)
    hbm = pl.BlockSpec(memory_space=pl.ANY)
    pairs = pltpu.SemaphoreType.DMA((2, RING, 2))
    return pl.pallas_call(
        kernel,
        out_shape=jax.ShapeDtypeStruct((SEQS, BLOCK, COLS), BF16),
        in_specs=[hbm] * 9,
        out_specs=pl.BlockSpec(memory_space=pltpu.VMEM),
        scratch_shapes=[
            pltpu.VMEM((SEQS, LOCAL_CH, BLOCK), BF16),
            pltpu.VMEM((PEERS * 32, 128), F32),
            pltpu.VMEM((1, LOCAL_CH), F32),
            pltpu.VMEM((2 * RES, 2 * PEERS), BF16),
            pltpu.VMEM((PEERS, 6 * RES), BF16),
            pltpu.VMEM((SEQS, LOCAL_CH, BLOCK), BF16),
            pltpu.VMEM((RING * RING * LOCAL_CH, COLS), BF16),
            pltpu.VMEM((4, BLOCK, BLOCK), BF16),
            pltpu.VMEM((2, RES, BLOCK), F32),
            pltpu.VMEM((4, SEQS * LOCAL_CH, 128), F32),
            pltpu.VMEM((4, SEQS * LOCAL_CH, 128), F32),
            pltpu.VMEM((4, SEQS * LOCAL_CH, 128), F32),
            pltpu.VMEM((2, RING * RING * LOCAL_CH, 128), F32),
            pltpu.VMEM((PEERS * 16, 128), F32),
            pltpu.VMEM((PEERS, 16, 128), BF16),
            pltpu.VMEM((PEERS, 16, 128), BF16),
            pltpu.VMEM((2, PEERS, 16, 128), BF16),
            pltpu.VMEM((2, PEERS, 16, 128), BF16),
            pltpu.VMEM((2, RES, BLOCK), F32),
            pltpu.VMEM((2, 8 * RES, BLOCK), F32),
            pltpu.VMEM((8 * RES, BLOCK), BF16),
            pltpu.VMEM((8 * RES, BLOCK), BF16),
            pltpu.VMEM((2, PEERS, 8, 128), BF16),
            pltpu.VMEM((2, PEERS, 8, 128), BF16),
            pltpu.VMEM((RING * RING, 2, 256, 128), BF16),
            pltpu.VMEM((RING * RING, 256, COLS), BF16),
            pltpu.VMEM((4 * 256, COLS), F32),
            pltpu.SemaphoreType.DMA((9,)),
            pltpu.SemaphoreType.DMA((5,)),
            pltpu.SemaphoreType.DMA((5,)),
            pairs, pairs, pairs, pairs, pairs, pairs,
        ],
        compiler_params=pltpu.CompilerParams(
            collective_id=0, has_side_effects=True, vmem_limit_bytes=62 * 1024 * 1024
        ),
    )(
        sequence, rows, skip.reshape(1, LOCAL_CH), jnp.asarray(first), jnp.asarray(last),
        gate, out_weight, jnp.asarray(dft), jnp.asarray(twiddle),
    )


def solution(mesh):
    in_specs = (
        P(None, "tensor", "context"),
        P(None, "tensor", "context"),
        P("tensor"),
        P(None, "tensor", "context", None),
        P(None, "tensor"),
    )
    out_specs = P(None, "context", "tensor")
    return jax.shard_map(local, mesh=mesh, in_specs=in_specs, out_specs=out_specs, check_vma=False)
```

time: 89.9 us -> 75.5 us (0.84)
  the two profiles are of different devices: /device:TPU:2 before, /device:TPU:1 now
where the time goes in v2:
time: 75.5 us; the launch traced here: 74.2 us
  Pallas kernels  72.4 us (96%)
  local copies, waits for them, and re-layouts  1.87 us (2%)
    pallas_call x1, Pallas kernels, local(): pl.pallas_call(kernel, out_shape=jax.ShapeDtypeStruct((SEQS, BLOCK, COLS)...  72.4 us
    unnamed x1, local copies, waits for them, and re-layouts  1.87 us

profile of v2, /device:TPU:1, one launch (start us, length us, event | category | flops | bytes accessed | tf_op | source)
XLA Modules:
  0.0 74.2 jit_solution(11922396974519370179)
XLA Ops:
  0.0 72.4 %shard_map.91 = bf16[2,512,256]{2,1,0:T(8,128)(2,1)} custom-call(bf16[2,64,512]{2,1,0:T(8,128)(2,1)} %seq_hbm.1, f32[1024,128]{1,0:T(8,128)} %bitcast.6, f32[1,64]{1,0:T(1,128)} %bitcast.7, bf16[128,64]{1,0:T(8,128)(2,1)} %constant.8.clone.first_hbm, bf16[32,384]{1,0:T(8,128)(2,1)} %constant.9.clone.last_hbm, bf16[2,64,512]{2,1,0:T(8,128)(2,1)} %gate_hbm.1, ...), custom_call_target="tpu_custom_call" | custom-call | tf_op jit(solution)/shard_map/pallas_call | solution.py:428
  72.4 1.9 %copy.12 = bf16[2,512,256]{2,1,0:T(8,128)(2,1)} copy(bf16[2,512,256]{2,1,0:T(8,128)(2,1)} %shard_map.91) | data formatting | bytes 1048576

commit v3 on v2

--- a/solution.py
+++ b/solution.py
@@ -63,25 +63,31 @@
     out_ref,
     seq, filt, skip, first, last, gate, w_rows, dft, tw,
     seq32, gate32, skipped, w32, msg32, sseq, rseq, sfilt, rfilt, spec, wide, lhs_hi, lhs_lo,
-    bsend, brecv, gbuf, wrep, acc,
-    load_sem, a2a_send, a2a_recv, z_send, z_recv, y_send, y_recv, h_send, h_recv,
+    bsend, brecv, mbuf, gbuf, wg, acc, osend,
+    load_sem, a2a_send, a2a_recv, w_send, w_recv, y_send, y_recv, z_send, z_recv, o_send, o_recv, o_own, far_sem,
 ):
     me = lax.axis_index("context")
     t = lax.axis_index("tensor")
     x, zh, core = me // 8, (me // 2) % 4, me % 2
     zl, y = t // RING, t % RING
-    right = zl * RING + (y + 1) % RING
-    left = zl * RING + (y + RING - 1) % RING
-
-    def over_peers(visit):
+    ring = zl * RING
+
+    def peers(lo, hi, visit):
         def step(j, carry):
+            steps = jnp.where(j < 8, 2, jnp.where(j < 16, 1, jnp.where(j < 24, 3, 0)))
             visit(
-                ((x + 2 + (j // 2) % 4) % 4) * 8 + ((zh + 2 + j // 8) % 4) * 2 + (core + j) % 2
+                ((x + 2 + (j // 2) % 4) % 4) * 8 + ((zh + steps) % 4) * 2 + (core + j) % 2
             )
             return carry
 
-        lax.fori_loop(0, 20, step, 0)
-        lax.fori_loop(21, PEERS, step, 0)
+        lax.fori_loop(lo, hi, step, 0)
+
+    def near_peers(visit):
+        peers(8, 28, visit)
+        peers(29, PEERS, visit)
+
+    def far_peers(visit):
+        peers(0, 8, visit)
 
     barrier = pltpu.get_barrier_semaphore()
 
@@ -90,17 +96,18 @@
             barrier, inc=1, device_id={"tensor": tensor, "context": context}, device_id_type=MESH
         )
 
-    over_peers(lambda peer: greet(t, peer))
-    greet(right, me)
-    greet(left, me)
-
-    @pl.when(zl < RING - 1)
-    def _():
-        greet(t + RING, me)
-
-    @pl.when(zl > 0)
-    def _():
-        greet(t - RING, me)
+    near_peers(lambda peer: greet(t, peer))
+    for k in range(1, RING):
+        greet(ring + (y + k) % RING, me)
+    for k in (1, 2):
+
+        @pl.when(zl < RING - k)
+        def _():
+            greet(t + k * RING, me)
+
+        @pl.when(zl >= k)
+        def _():
+            greet(t - k * RING, me)
 
     loads = [
         pltpu.make_async_copy(src, dst, load_sem.at[i])
@@ -130,10 +137,18 @@
     for chl in range(2):
         sfilt[chl] = jnp.concatenate([parts[0, :, chl], parts[1, :, chl]], axis=1).astype(BF16)
 
-    z_neighbours = jnp.where(zl < RING - 1, 1, 0) + jnp.where(zl > 0, 1, 0)
-    pl.semaphore_wait(barrier, PEERS - 1 + 2 + z_neighbours)
-
-    def exchange(src, dst, sem):
+    z_neighbours = jnp.where((zl == 0) | (zl == RING - 1), 2, 3)
+    pl.semaphore_wait(barrier, 23 + 3 + z_neighbours)
+    next_up, next_down = (
+        x * 8 + ((zh + 1) % 4) * 2 + core,
+        x * 8 + ((zh + 3) % 4) * 2 + core,
+    )
+    for peer in (next_up, next_down):
+        pl.semaphore_signal(
+            far_sem, inc=1, device_id={"tensor": t, "context": peer}, device_id_type=MESH
+        )
+
+    def sender(src, dst, sem):
         def send(peer):
             pltpu.make_async_remote_copy(
                 src_ref=src.at[peer],
@@ -144,15 +159,25 @@
                 device_id_type=MESH,
             ).start()
 
-        over_peers(send)
+        return send
+
+    def exchange(src, dst, sem):
+        send = sender(src, dst, sem)
+        far_peers(send)
+        near_peers(send)
         dst[me] = src[me]
 
     def wait_all(buf, sem):
         view = buf.at[pl.ds(0, PEERS - 1)]
         pltpu.make_async_copy(view, view, sem).wait()
 
-    exchange(sseq, rseq, 0)
-    exchange(sfilt.at[0], rfilt.at[0], 1)
+    early = ((sseq, rseq, 0), (sfilt.at[0], rfilt.at[0], 1))
+    for src, dst, sem in early:
+        near_peers(sender(src, dst, sem))
+        dst[me] = src[me]
+    pl.semaphore_wait(far_sem, 2)
+    for src, dst, sem in early:
+        far_peers(sender(src, dst, sem))
     exchange(sfilt.at[1], rfilt.at[1], 2)
 
     for load in loads[2:]:
@@ -172,8 +197,20 @@
         for tt in range(RING * RING):
             for chl in range(2):
                 rows = w32[half, pl.ds(tt * LOCAL_CH + chl, PEERS, stride=2), :].astype(BF16)
-                for copy_of in range(4):
-                    wrep[tt, pl.ds(chl * 128 + copy_of * PEERS, PEERS), lanes] = rows
+                wg[y, tt, chl, :, lanes] = rows
+    w_copies = [
+        pltpu.make_async_remote_copy(
+            src_ref=wg.at[y],
+            dst_ref=wg.at[y],
+            send_sem=w_send.at[k - 1],
+            recv_sem=w_recv.at[k - 1],
+            device_id={"tensor": ring + (y + k) % RING, "context": me},
+            device_id_type=MESH,
+        )
+        for k in range(1, RING)
+    ]
+    for c in w_copies:
+        c.start()
 
     wait_all(rseq, a2a_recv.at[0])
     msg32[...] = rseq[...].reshape(PEERS * 16, 128).astype(F32)
@@ -239,197 +276,168 @@
         bsend[chl] = msg32[pl.ds(0, PEERS * 8), :].reshape(PEERS, 8, 128).astype(BF16)
         exchange(bsend.at[chl], brecv.at[chl], 3 + chl)
 
+    def quarter_copy(chl, k):
+        return pltpu.make_async_remote_copy(
+            src_ref=mbuf.at[chl, (y + k) % RING],
+            dst_ref=gbuf.at[zl, chl, y],
+            send_sem=y_send.at[chl, k - 1],
+            recv_sem=y_recv.at[chl],
+            device_id={"tensor": ring + (y + k) % RING, "context": me},
+            device_id_type=MESH,
+        )
+
     def mix(chl):
         wait_all(brecv.at[chl], a2a_recv.at[3 + chl])
         msg32[pl.ds(0, PEERS * 8), :] = brecv[chl].astype(F32).reshape(PEERS * 8, 128)
-        for block in range(2):
+        for bh in range(4):
             pieces = []
-            for half in range(2):
-                bh = half * 2 + block
-                for s in range(SEQS):
-                    rows = pl.ds(s * LOCAL_CH + chl, PEERS, stride=2)
-                    conv = msg32[pl.ds(s * 4 + bh, PEERS, stride=8), :]
-                    pieces.append(gate32[bh, rows, :] * (conv + skipped[bh, rows, :]))
-            mixed = jnp.concatenate(pieces, axis=0)
-            gbuf[t, chl, pl.ds(block * 128, 128), :] = mixed.T.astype(BF16)
-
-    def copy(slot, chl, rows, send_sem, recv_sem, target):
-        ref = gbuf.at[slot, chl, rows]
+            for s in range(SEQS):
+                rows = pl.ds(s * LOCAL_CH + chl, PEERS, stride=2)
+                conv = msg32[pl.ds(s * 4 + bh, PEERS, stride=8), :]
+                pieces.append(gate32[bh, rows, :] * (conv + skipped[bh, rows, :]))
+            for s in range(SEQS):
+                mbuf[chl, bh, s] = pieces[s].astype(BF16)
+        for k in range(1, RING):
+            quarter_copy(chl, k).start()
+        gbuf[zl, chl, y] = mbuf[chl, y]
+
+    def z_copy(origin, part, slot, target):
+        ref = gbuf.at[origin, 0] if part == 0 else gbuf.at[origin, 1, :, part - 1]
         return pltpu.make_async_remote_copy(
             src_ref=ref,
             dst_ref=ref,
-            send_sem=send_sem,
-            recv_sem=recv_sem,
+            send_sem=z_send.at[part, slot],
+            recv_sem=z_recv.at[part, origin],
             device_id={"tensor": target, "context": me},
             device_id_type=MESH,
         )
 
-    whole, front, back = pl.ds(0, 256), pl.ds(0, 128), pl.ds(128, 128)
-    beyond_left, beyond_right = (y + RING - 1) % RING, (y + 1) % RING
-
-    def up(k, chl):
-        return copy(t - k * RING, chl, whole, z_send.at[0, k, chl], z_recv.at[0, k, chl], t + RING)
-
-    def down(k, chl):
-        return copy(t + k * RING, chl, whole, z_send.at[1, k, chl], z_recv.at[1, k, chl], t - RING)
-
-    def y_copies(z, chl, column_right=None, column_left=None):
-        return (
-            copy(z * RING + (y if column_right is None else column_right), chl, whole,
-                 y_send.at[0, z, chl], y_recv.at[0, z, chl], right),
-            copy(z * RING + (y if column_left is None else column_left), chl, whole,
-                 y_send.at[1, z, chl], y_recv.at[1, z, chl], left),
-        )
-
-    def y_halves(z, chl, column_right, column_left):
-        return (
-            copy(z * RING + column_right, chl, front, h_send.at[0, z, chl], h_recv.at[0, z, chl], right),
-            copy(z * RING + column_left, chl, back, h_send.at[1, z, chl], h_recv.at[1, z, chl], left),
-        )
-
-    def start_own(chl):
-        @pl.when(zl < RING - 1)
+    inner_chip = (zl == 1) | (zl == 2)
+    partner = (zl + 1 - 2 * (zl % 2), (zl + 2) % RING, RING - 1 - zl)
+
+    def z_sends(part, visit):
+        for k in (2, 1):
+
+            @pl.when(zl < RING - k)
+            def _():
+                visit(z_copy(zl, part, 2 * k - 2, t + k * RING))
+
+            @pl.when(zl >= k)
+            def _():
+                visit(z_copy(zl, part, 2 * k - 1, t - k * RING))
+
+    def pass_on(part):
+        return z_copy(partner[1], part, 4, t + (2 * zl - 3) * RING)
+
+    def wait_quarters(chl):
+        view = gbuf.at[0, chl, pl.ds(0, RING - 1)]
+        pltpu.make_async_copy(view, view, y_recv.at[chl]).wait()
+
+    def z_wait(part, k):
+        z_copy(partner[k - 1], part, 0, t).wait_recv()
+        if k == 2:
+
+            @pl.when(inner_chip)
+            def _():
+                pass_on(part).start()
+
+    def tokens_of(z, chl, s):
+        return gbuf[z, chl, :, s].astype(F32).reshape(128, 128).T.astype(BF16)
+
+    def weights_of(z, chl, column):
+        return jnp.concatenate([wg[column, z * RING + yy, chl] for yy in range(RING)], axis=0)
+
+    def project(chl, s, items):
+        lhs = jnp.concatenate([tokens_of(z, chl, s) for z in items], axis=1)
+
+        def columns(column):
+            return dot(lhs, jnp.concatenate([weights_of(z, chl, column) for z in items], axis=0))
+
+        return columns
+
+    def result_copy(s, k):
+        column = (y + k) % RING
+        return pltpu.make_async_remote_copy(
+            src_ref=osend.at[s, column],
+            dst_ref=out_ref.at[s, pl.ds(y * 128, 128), :],
+            send_sem=o_send.at[s, k - 1],
+            recv_sem=o_recv.at[s, k - 1],
+            device_id={"tensor": ring + column, "context": me},
+            device_id_type=MESH,
+        )
+
+    def own_result(s):
+        return pltpu.make_async_copy(
+            osend.at[s, y], out_ref.at[s, pl.ds(y * 128, 128), :], o_own.at[s]
+        )
+
+    mix(0)
+    wait_quarters(0)
+    z_sends(0, lambda c: c.start())
+    mix(1)
+    wait_quarters(1)
+    for s in range(SEQS):
+        z_sends(1 + s, lambda c: c.start())
+    z_wait(0, 2)
+    z_wait(0, 1)
+    for c in w_copies:
+        c.wait_recv()
+    for s in range(SEQS):
+        near = project(0, s, (zl, partner[0]))
+        for column in range(RING):
+            acc[s, column] = near(column)
+    z_wait(1, 2)
+    z_wait(0, 3)
+    for s in range(SEQS):
+        far = project(0, s, (partner[1], partner[2]))
+        for column in range(RING):
+            acc[s, column] += far(column)
+    z_wait(2, 2)
+    for s in range(SEQS):
+        z_wait(1 + s, 1)
+        near = project(1, s, (zl, partner[0]))
+        for column in range(RING):
+            acc[s, column] += near(column)
+        z_wait(1 + s, 3)
+        far = project(1, s, (partner[1], partner[2]))
+        for k in (2, 1, 3, 0):
+            column = (y + k) % RING
+            osend[s, column] = (acc[s, column] + far(column)).astype(BF16)
+            if k:
+                result_copy(s, k).start()
+            else:
+                own_result(s).start()
+    for s in range(SEQS):
+        own_result(s).wait()
+        for k in range(1, RING):
+            result_copy(s, k).wait_recv()
+
+    for part in range(3):
+        z_sends(part, lambda c: c.wait_send())
+
+        @pl.when(inner_chip)
         def _():
-            up(0, chl).start()
-
-        @pl.when(zl > 0)
-        def _():
-            down(0, chl).start()
-
-        for c in y_copies(zl, chl):
-            c.start()
-
-    def on_levels(k, visit):
-        if k == 0:
-            visit(zl)
-            return
-
-        @pl.when(zl >= k)
-        def _():
-            visit(zl - k)
-
-        @pl.when(zl < RING - k)
-        def _():
-            visit(zl + k)
-
-    def z_step(k, chl):
-        @pl.when(zl >= k)
-        def _():
-            copy(t - k * RING, chl, whole, z_send.at[0, k - 1, chl], z_recv.at[0, k - 1, chl], t).wait_recv()
-
-            @pl.when(zl < RING - 1)
-            def _():
-                up(k, chl).start()
-
-            for c in y_copies(zl - k, chl):
-                c.start()
-
-        @pl.when(zl < RING - k)
-        def _():
-            copy(t + k * RING, chl, whole, z_send.at[1, k - 1, chl], z_recv.at[1, k - 1, chl], t).wait_recv()
-
-            @pl.when(zl > 0)
-            def _():
-                down(k, chl).start()
-
-            for c in y_copies(zl + k, chl):
-                c.start()
-
-    def y_step(k, chl):
-        def visit(z):
-            for arrived, half in zip(
-                y_copies(z, chl, beyond_left, beyond_right), y_halves(z, chl, beyond_left, beyond_right)
-            ):
-                arrived.wait_recv()
-                half.start()
-
-        on_levels(k, visit)
-
-    lane_group = lax.broadcasted_iota(jnp.int32, (256, 2 * 128), 1) % 128 // PEERS
-
-    def project(slot):
-        both = jnp.concatenate([gbuf[slot, 0], gbuf[slot, 1]], axis=1)
-        stacked = jnp.concatenate(
-            [jnp.where(lane_group == group, both, jnp.zeros_like(both)) for group in range(4)], axis=0
-        )
-        acc[...] += dot(stacked, wrep[slot])
-
-    def project_near(k):
-        def visit(z):
-            for column in (y, beyond_left, beyond_right):
-                project(z * RING + column)
-
-        on_levels(k, visit)
-
-    def project_far(k):
-        def visit(z):
-            column = (y + 2) % RING
-            for chl in range(2):
-                for c in y_halves(z, chl, column, column):
-                    c.wait_recv()
-            project(z * RING + column)
-
-        on_levels(k, visit)
-
-    acc[...] = jnp.zeros_like(acc)
-    mix(0)
-    start_own(0)
-    z_step(1, 0)
-    y_step(0, 0)
-    mix(1)
-    start_own(1)
-    z_step(2, 0)
-    y_step(1, 0)
-    z_step(1, 1)
-    y_step(0, 1)
-    z_step(3, 0)
-    y_step(2, 0)
-    z_step(2, 1)
-    y_step(1, 1)
-    project_near(0)
-    z_step(3, 1)
-    y_step(3, 0)
-    y_step(2, 1)
-    project_near(1)
-    y_step(3, 1)
-    project_far(0)
-    project_near(2)
-    project_far(1)
-    project_near(3)
-    project_far(2)
-    project_far(3)
-
-    for group in range(4):
-        out_ref[group % 2, pl.ds(group // 2 * 256, 256), :] = acc[pl.ds(group * 256, 256), :].astype(BF16)
-
+            pass_on(part).wait_send()
+
+    for k in range(1, RING):
+        w_copies[k - 1].wait_send()
+        for s in range(SEQS):
+            result_copy(s, k).wait_send()
+        for chl in range(2):
+            quarter_copy(chl, k).wait_send()
     for i, buf in enumerate((sseq, sfilt.at[0], sfilt.at[1], bsend.at[0], bsend.at[1])):
         wait_all(buf, a2a_send.at[i])
-    for chl in range(2):
-        for k in range(RING - 1):
-
-            @pl.when((zl >= k) & (zl < RING - 1))
-            def _():
-                up(k, chl).wait_send()
-
-            @pl.when((zl < RING - k) & (zl > 0))
-            def _():
-                down(k, chl).wait_send()
-
-        for z in range(RING):
-            for c in y_copies(z, chl) + y_halves(z, chl, y, y):
-                c.wait_send()
 
 
 def local(sequence, gate, skip, filter_spectrum, out_weight):
     first, last, dft, twiddle = tables()
     rows = filter_spectrum.reshape(2, LOCAL_CH, 2, 4, 128).transpose(0, 1, 3, 2, 4).reshape(-1, 128)
     hbm = pl.BlockSpec(memory_space=pl.ANY)
-    pairs = pltpu.SemaphoreType.DMA((2, RING, 2))
     return pl.pallas_call(
         kernel,
         out_shape=jax.ShapeDtypeStruct((SEQS, BLOCK, COLS), BF16),
         in_specs=[hbm] * 9,
-        out_specs=pl.BlockSpec(memory_space=pltpu.VMEM),
+        out_specs=hbm,
         scratch_shapes=[
             pltpu.VMEM((SEQS, LOCAL_CH, BLOCK), BF16),
             pltpu.VMEM((PEERS * 32, 128), F32),
@@ -455,13 +463,24 @@
             pltpu.VMEM((8 * RES, BLOCK), BF16),
             pltpu.VMEM((2, PEERS, 8, 128), BF16),
             pltpu.VMEM((2, PEERS, 8, 128), BF16),
-            pltpu.VMEM((RING * RING, 2, 256, 128), BF16),
-            pltpu.VMEM((RING * RING, 256, COLS), BF16),
-            pltpu.VMEM((4 * 256, COLS), F32),
+            pltpu.VMEM((2, RING, SEQS, PEERS, 128), BF16),
+            pltpu.VMEM((RING, 2, RING, SEQS, PEERS, 128), BF16),
+            pltpu.VMEM((RING, RING * RING, 2, PEERS, COLS), BF16),
+            pltpu.VMEM((SEQS, RING, 128, COLS), F32),
+            pltpu.VMEM((SEQS, RING, 128, COLS), BF16),
             pltpu.SemaphoreType.DMA((9,)),
             pltpu.SemaphoreType.DMA((5,)),
             pltpu.SemaphoreType.DMA((5,)),
-            pairs, pairs, pairs, pairs, pairs, pairs,
+            pltpu.SemaphoreType.DMA((RING - 1,)),
+            pltpu.SemaphoreType.DMA((RING - 1,)),
+            pltpu.SemaphoreType.DMA((2, RING - 1)),
+            pltpu.SemaphoreType.DMA((2,)),
+            pltpu.SemaphoreType.DMA((3, 5)),
+            pltpu.SemaphoreType.DMA((3, RING)),
+            pltpu.SemaphoreType.DMA((SEQS, RING - 1)),
+            pltpu.SemaphoreType.DMA((SEQS, RING - 1)),
+            pltpu.SemaphoreType.DMA((SEQS,)),
+            pltpu.SemaphoreType.REGULAR,
         ],
         compiler_params=pltpu.CompilerParams(
             collective_id=0, has_side_effects=True, vmem_limit_bytes=62 * 1024 * 1024

time: 75.5 us -> 68.8 us (0.911)
  Pallas kernels: 72.4 us -> 66.4 us
    pallas_call x1, Pallas kernels: 72.4 us -> 66.4 us  [local(): pl.pallas_call(kernel, out_shape=jax.ShapeDtypeStruct((SEQS, BLOCK, COLS)...]
where the time goes in v3:
time: 68.8 us; the launch traced here: 68.3 us
  Pallas kernels  66.4 us (97%)
  local copies, waits for them, and re-layouts  1.87 us (3%)
    pallas_call x1, Pallas kernels, local(): pl.pallas_call(kernel, out_shape=jax.ShapeDtypeStruct((SEQS, BLOCK, COLS)...  66.4 us
    unnamed x1, local copies, waits for them, and re-layouts  1.87 us

profile of v3, /device:TPU:1, one launch (start us, length us, event | category | flops | bytes accessed | tf_op | source)
XLA Modules:
  0.0 68.3 jit_solution(11926435507427015619)
XLA Ops:
  0.0 66.4 %shard_map.91 = bf16[2,512,256]{2,1,0:T(8,128)(2,1)} custom-call(bf16[2,64,512]{2,1,0:T(8,128)(2,1)} %seq_hbm.1, f32[1024,128]{1,0:T(8,128)} %bitcast.6, f32[1,64]{1,0:T(1,128)} %bitcast.7, bf16[128,64]{1,0:T(8,128)(2,1)} %constant.8.clone.first_hbm, bf16[32,384]{1,0:T(8,128)(2,1)} %constant.9.clone.last_hbm, bf16[2,64,512]{2,1,0:T(8,128)(2,1)} %gate_hbm.1, ...), custom_call_target="tpu_custom_call" | custom-call | tf_op jit(solution)/shard_map/pallas_call | solution.py:436
  66.4 1.9 %copy.12 = bf16[2,512,256]{2,1,0:T(8,128)(2,1)} copy(bf16[2,512,256]{2,1,0:T(8,128)(2,1)} %shard_map.91) | data formatting | bytes 1048576

commit v4 on v3

--- a/solution.py
+++ b/solution.py
@@ -89,26 +89,6 @@
     def far_peers(visit):
         peers(0, 8, visit)
 
-    barrier = pltpu.get_barrier_semaphore()
-
-    def greet(tensor, context):
-        pl.semaphore_signal(
-            barrier, inc=1, device_id={"tensor": tensor, "context": context}, device_id_type=MESH
-        )
-
-    near_peers(lambda peer: greet(t, peer))
-    for k in range(1, RING):
-        greet(ring + (y + k) % RING, me)
-    for k in (1, 2):
-
-        @pl.when(zl < RING - k)
-        def _():
-            greet(t + k * RING, me)
-
-        @pl.when(zl >= k)
-        def _():
-            greet(t - k * RING, me)
-
     loads = [
         pltpu.make_async_copy(src, dst, load_sem.at[i])
         for i, (src, dst) in enumerate(
@@ -118,7 +98,30 @@
             ]
         )
     ]
-    for load in loads:
+    for load in loads[:2]:
+        load.start()
+
+    barrier = pltpu.get_barrier_semaphore()
+
+    def greet(tensor, context):
+        pl.semaphore_signal(
+            barrier, inc=1, device_id={"tensor": tensor, "context": context}, device_id_type=MESH
+        )
+
+    near_peers(lambda peer: greet(t, peer))
+    for k in range(1, RING):
+        greet(ring + (y + k) % RING, me)
+    for k in (1, 2):
+
+        @pl.when(zl < RING - k)
+        def _():
+            greet(t + k * RING, me)
+
+        @pl.when(zl >= k)
+        def _():
+            greet(t - k * RING, me)
+
+    for load in loads[2:]:
         load.start()
 
     loads[0].wait()
@@ -132,11 +135,6 @@
                     bh, pl.ds(s * LOCAL_CH + chl, PEERS, stride=2), :
                 ]
     sseq[...] = msg32[...].reshape(PEERS, 16, 128).astype(BF16)
-    loads[1].wait()
-    parts = filt[...].reshape(2, PEERS, 2, 8, 128)
-    for chl in range(2):
-        sfilt[chl] = jnp.concatenate([parts[0, :, chl], parts[1, :, chl]], axis=1).astype(BF16)
-
     z_neighbours = jnp.where((zl == 0) | (zl == RING - 1), 2, 3)
     pl.semaphore_wait(barrier, 23 + 3 + z_neighbours)
     next_up, next_down = (
@@ -171,10 +169,15 @@
         view = buf.at[pl.ds(0, PEERS - 1)]
         pltpu.make_async_copy(view, view, sem).wait()
 
+    near_peers(sender(sseq, rseq, 0))
+    rseq[me] = sseq[me]
+    loads[1].wait()
+    parts = filt[...].reshape(2, PEERS, 2, 8, 128)
+    for chl in range(2):
+        sfilt[chl] = jnp.concatenate([parts[0, :, chl], parts[1, :, chl]], axis=1).astype(BF16)
     early = ((sseq, rseq, 0), (sfilt.at[0], rfilt.at[0], 1))
-    for src, dst, sem in early:
-        near_peers(sender(src, dst, sem))
-        dst[me] = src[me]
+    near_peers(sender(*early[1]))
+    rfilt[0, me] = sfilt[0, me]
     pl.semaphore_wait(far_sem, 2)
     for src, dst, sem in early:
         far_peers(sender(src, dst, sem))
@@ -232,14 +235,13 @@
                 lhs_lo[pl.ds(base(chl, part, s), RES), :] = lo
 
     def inner(which, rows):
-        hi, lo = lhs_hi[rows, :], lhs_lo[rows, :]
-        return dot(hi, dft[2 * which]) + dot(lo, dft[2 * which]) + dot(hi, dft[2 * which + 1])
-
-    everything = pl.ds(0, 8 * RES)
-    wide[0] = inner(0, everything)
-    wide[1] = inner(1, everything)
+        hi = lhs_hi[rows, :]
+        return dot(hi, dft[2 * which]) + dot(hi, dft[2 * which + 1])
 
     for chl in range(2):
+        channel = pl.ds(chl * 4 * RES, 4 * RES)
+        for which in range(2):
+            wide[which] = inner(which, channel) + dot(lhs_lo[channel, :], dft[2 * which])
         wait_all(rfilt.at[chl], a2a_recv.at[1 + chl])
         msg32[...] = rfilt[chl].reshape(PEERS * 16, 128).astype(F32)
         for ri in range(2):
@@ -249,21 +251,15 @@
                         pl.ds(ri * 8 + mh * 2 + j, PEERS, stride=16), :
                     ]
         for s in range(SEQS):
-            rows, rows_im = pl.ds(base(chl, 0, s), RES), pl.ds(base(chl, 1, s), RES)
+            rows, rows_im = pl.ds(s * RES, RES), pl.ds((2 + s) * RES, RES)
             f_re = wide[0, rows, :] + wide[1, rows_im, :]
             f_im = wide[0, rows_im, :] - wide[1, rows, :]
-            for which, value in (
-                (rows, f_re * spec[0] - f_im * spec[1]),
-                (rows_im, f_re * spec[1] + f_im * spec[0]),
-            ):
-                hi, lo = split(value)
-                lhs_hi[which, :] = hi
-                lhs_lo[which, :] = lo
-        channel = pl.ds(chl * 4 * RES, 4 * RES)
-        wide[0, channel, :] = inner(0, channel)
-        wide[1, channel, :] = inner(1, channel)
+            lhs_hi[pl.ds(base(chl, 0, s), RES), :] = (f_re * spec[0] - f_im * spec[1]).astype(BF16)
+            lhs_hi[pl.ds(base(chl, 1, s), RES), :] = (f_re * spec[1] + f_im * spec[0]).astype(BF16)
+        for which in range(2):
+            wide[which] = inner(which, channel)
         for s in range(SEQS):
-            rows, rows_im = pl.ds(base(chl, 0, s), RES), pl.ds(base(chl, 1, s), RES)
+            rows, rows_im = pl.ds(s * RES, RES), pl.ds((2 + s) * RES, RES)
             b_re = wide[0, rows, :] - wide[1, rows_im, :]
             b_im = wide[0, rows_im, :] + wide[1, rows, :]
             re_hi, re_lo = split(b_re * tw[0] - b_im * tw[1])
@@ -279,7 +275,7 @@
     def quarter_copy(chl, k):
         return pltpu.make_async_remote_copy(
             src_ref=mbuf.at[chl, (y + k) % RING],
-            dst_ref=gbuf.at[zl, chl, y],
+            dst_ref=gbuf.at[zl, chl, RING - k],
             send_sem=y_send.at[chl, k - 1],
             recv_sem=y_recv.at[chl],
             device_id={"tensor": ring + (y + k) % RING, "context": me},
@@ -297,12 +293,19 @@
                 pieces.append(gate32[bh, rows, :] * (conv + skipped[bh, rows, :]))
             for s in range(SEQS):
                 mbuf[chl, bh, s] = pieces[s].astype(BF16)
-        for k in range(1, RING):
+        for k in (2, 1, 3):
             quarter_copy(chl, k).start()
-        gbuf[zl, chl, y] = mbuf[chl, y]
+        gbuf[zl, chl, 0] = mbuf[chl, y]
 
     def z_copy(origin, part, slot, target):
-        ref = gbuf.at[origin, 0] if part == 0 else gbuf.at[origin, 1, :, part - 1]
+        others = pl.ds(1, RING - 1)
+        ref = (
+            gbuf.at[origin, 0, 0],
+            gbuf.at[origin, 0, others],
+            gbuf.at[origin, 1, 0],
+            gbuf.at[origin, 1, others, 0],
+            gbuf.at[origin, 1, others, 1],
+        )[part]
         return pltpu.make_async_remote_copy(
             src_ref=ref,
             dst_ref=ref,
@@ -345,7 +348,9 @@
         return gbuf[z, chl, :, s].astype(F32).reshape(128, 128).T.astype(BF16)
 
     def weights_of(z, chl, column):
-        return jnp.concatenate([wg[column, z * RING + yy, chl] for yy in range(RING)], axis=0)
+        return jnp.concatenate(
+            [wg[column, z * RING + (y + r) % RING, chl] for r in range(RING)], axis=0
+        )
 
     def project(chl, s, items):
         lhs = jnp.concatenate([tokens_of(z, chl, s) for z in items], axis=1)
@@ -371,34 +376,45 @@
             osend.at[s, y], out_ref.at[s, pl.ds(y * 128, 128), :], o_own.at[s]
         )
 
+    def start(part):
+        z_sends(part, lambda c: c.start())
+
     mix(0)
+    start(0)
     wait_quarters(0)
-    z_sends(0, lambda c: c.start())
+    start(1)
     mix(1)
+    start(2)
+    z_wait(0, 2)
     wait_quarters(1)
-    for s in range(SEQS):
-        z_sends(1 + s, lambda c: c.start())
-    z_wait(0, 2)
+    start(3)
+    start(4)
+    z_wait(1, 2)
+    z_wait(2, 2)
     z_wait(0, 1)
+    z_wait(1, 1)
     for c in w_copies:
         c.wait_recv()
     for s in range(SEQS):
         near = project(0, s, (zl, partner[0]))
         for column in range(RING):
             acc[s, column] = near(column)
-    z_wait(1, 2)
+    z_wait(3, 2)
     z_wait(0, 3)
+    z_wait(1, 3)
     for s in range(SEQS):
         far = project(0, s, (partner[1], partner[2]))
         for column in range(RING):
             acc[s, column] += far(column)
-    z_wait(2, 2)
-    for s in range(SEQS):
-        z_wait(1 + s, 1)
+    z_wait(4, 2)
+    z_wait(2, 1)
+    z_wait(2, 3)
+    for s in range(SEQS):
+        z_wait(3 + s, 1)
         near = project(1, s, (zl, partner[0]))
         for column in range(RING):
             acc[s, column] += near(column)
-        z_wait(1 + s, 3)
+        z_wait(3 + s, 3)
         far = project(1, s, (partner[1], partner[2]))
         for k in (2, 1, 3, 0):
             column = (y + k) % RING
@@ -412,7 +428,7 @@
         for k in range(1, RING):
             result_copy(s, k).wait_recv()
 
-    for part in range(3):
+    for part in range(5):
         z_sends(part, lambda c: c.wait_send())
 
         @pl.when(inner_chip)
@@ -458,7 +474,7 @@
             pltpu.VMEM((2, PEERS, 16, 128), BF16),
             pltpu.VMEM((2, PEERS, 16, 128), BF16),
             pltpu.VMEM((2, RES, BLOCK), F32),
-            pltpu.VMEM((2, 8 * RES, BLOCK), F32),
+            pltpu.VMEM((2, 4 * RES, BLOCK), F32),
             pltpu.VMEM((8 * RES, BLOCK), BF16),
             pltpu.VMEM((8 * RES, BLOCK), BF16),
             pltpu.VMEM((2, PEERS, 8, 128), BF16),
@@ -475,8 +491,8 @@
             pltpu.SemaphoreType.DMA((RING - 1,)),
             pltpu.SemaphoreType.DMA((2, RING - 1)),
             pltpu.SemaphoreType.DMA((2,)),
-            pltpu.SemaphoreType.DMA((3, 5)),
-            pltpu.SemaphoreType.DMA((3, RING)),
+            pltpu.SemaphoreType.DMA((5, 5)),
+            pltpu.SemaphoreType.DMA((5, RING)),
             pltpu.SemaphoreType.DMA((SEQS, RING - 1)),
             pltpu.SemaphoreType.DMA((SEQS, RING - 1)),
             pltpu.SemaphoreType.DMA((SEQS,)),

time: 68.8 us -> 66.5 us (0.967)
  Pallas kernels: 66.4 us -> 64.2 us
    pallas_call x1, Pallas kernels: 66.4 us -> 64.2 us  [local(): pl.pallas_call(kernel, out_shape=jax.ShapeDtypeStruct((SEQS, BLOCK, COLS)...]
where the time goes in v4:
time: 66.5 us; the launch traced here: 66 us
  Pallas kernels  64.2 us (97%)
  local copies, waits for them, and re-layouts  1.87 us (3%)
    pallas_call x1, Pallas kernels, local(): pl.pallas_call(kernel, out_shape=jax.ShapeDtypeStruct((SEQS, BLOCK, COLS)...  64.2 us
    unnamed x1, local copies, waits for them, and re-layouts  1.87 us

profile of v4, /device:TPU:1, one launch (start us, length us, event | category | flops | bytes accessed | tf_op | source)
XLA Modules:
  0.0 66.0 jit_solution(625338730996401714)
XLA Ops:
  0.0 64.2 %shard_map.91 = bf16[2,512,256]{2,1,0:T(8,128)(2,1)} custom-call(bf16[2,64,512]{2,1,0:T(8,128)(2,1)} %seq_hbm.1, f32[1024,128]{1,0:T(8,128)} %bitcast.6, f32[1,64]{1,0:T(1,128)} %bitcast.7, bf16[128,64]{1,0:T(8,128)(2,1)} %constant.8.clone.first_hbm, bf16[32,384]{1,0:T(8,128)(2,1)} %constant.9.clone.last_hbm, bf16[2,64,512]{2,1,0:T(8,128)(2,1)} %gate_hbm.1, ...), custom_call_target="tpu_custom_call" | custom-call | tf_op jit(solution)/shard_map/pallas_call | solution.py:452
  64.2 1.9 %copy.12 = bf16[2,512,256]{2,1,0:T(8,128)(2,1)} copy(bf16[2,512,256]{2,1,0:T(8,128)(2,1)} %shard_map.91) | data formatting | bytes 1048576

commit v5 on v4

--- a/solution.py
+++ b/solution.py
@@ -134,7 +134,7 @@
                 msg32[pl.ds((s * 2 + chl) * 4 + bh, PEERS, stride=16), :] = seq32[
                     bh, pl.ds(s * LOCAL_CH + chl, PEERS, stride=2), :
                 ]
-    sseq[...] = msg32[...].reshape(PEERS, 16, 128).astype(BF16)
+    sseq[...] = msg32[pl.ds(0, PEERS * 16), :].reshape(PEERS, 16, 128).astype(BF16)
     z_neighbours = jnp.where((zl == 0) | (zl == RING - 1), 2, 3)
     pl.semaphore_wait(barrier, 23 + 3 + z_neighbours)
     next_up, next_down = (
@@ -196,7 +196,7 @@
             gate32[bh, rows, :] = gate[s, :, pl.ds(bh * 128, 128)].astype(F32)
     for half in range(2):
         lanes = pl.ds(half * 128, 128)
-        w32[half] = w_rows[:, lanes].astype(F32)
+        w32[half, pl.ds(0, RING * RING * LOCAL_CH), :] = w_rows[:, lanes].astype(F32)
         for tt in range(RING * RING):
             for chl in range(2):
                 rows = w32[half, pl.ds(tt * LOCAL_CH + chl, PEERS, stride=2), :].astype(BF16)
@@ -216,7 +216,7 @@
         c.start()
 
     wait_all(rseq, a2a_recv.at[0])
-    msg32[...] = rseq[...].reshape(PEERS * 16, 128).astype(F32)
+    msg32[pl.ds(0, PEERS * 16), :] = rseq[...].reshape(PEERS * 16, 128).astype(F32)
 
     def base(chl, part, s):
         return ((chl * 2 + part) * 2 + s) * RES
@@ -243,7 +243,7 @@
         for which in range(2):
             wide[which] = inner(which, channel) + dot(lhs_lo[channel, :], dft[2 * which])
         wait_all(rfilt.at[chl], a2a_recv.at[1 + chl])
-        msg32[...] = rfilt[chl].reshape(PEERS * 16, 128).astype(F32)
+        msg32[pl.ds(0, PEERS * 16), :] = rfilt[chl].reshape(PEERS * 16, 128).astype(F32)
         for ri in range(2):
             for j in range(2):
                 for mh in range(4):
@@ -464,11 +464,11 @@
             pltpu.VMEM((RING * RING * LOCAL_CH, COLS), BF16),
             pltpu.VMEM((4, BLOCK, BLOCK), BF16),
             pltpu.VMEM((2, RES, BLOCK), F32),
-            pltpu.VMEM((4, SEQS * LOCAL_CH, 128), F32),
-            pltpu.VMEM((4, SEQS * LOCAL_CH, 128), F32),
-            pltpu.VMEM((4, SEQS * LOCAL_CH, 128), F32),
-            pltpu.VMEM((2, RING * RING * LOCAL_CH, 128), F32),
-            pltpu.VMEM((PEERS * 16, 128), F32),
+            pltpu.VMEM((4, SEQS * LOCAL_CH + 8, 128), F32),
+            pltpu.VMEM((4, SEQS * LOCAL_CH + 8, 128), F32),
+            pltpu.VMEM((4, SEQS * LOCAL_CH + 8, 128), F32),
+            pltpu.VMEM((2, RING * RING * LOCAL_CH + 8, 128), F32),
+            pltpu.VMEM((PEERS * 16 + 16, 128), F32),
             pltpu.VMEM((PEERS, 16, 128), BF16),
             pltpu.VMEM((PEERS, 16, 128), BF16),
             pltpu.VMEM((2, PEERS, 16, 128), BF16),

time: 66.5 us -> 67.7 us (1.018)
  Pallas kernels: 64.2 us -> 65.7 us
    pallas_call x1, Pallas kernels: 64.2 us -> 65.7 us  [local(): pl.pallas_call(kernel, out_shape=jax.ShapeDtypeStruct((SEQS, BLOCK, COLS)...]
where the time goes in v5:
time: 67.7 us; the launch traced here: 67.5 us
  Pallas kernels  65.7 us (97%)
  local copies, waits for them, and re-layouts  1.87 us (3%)
    pallas_call x1, Pallas kernels, local(): pl.pallas_call(kernel, out_shape=jax.ShapeDtypeStruct((SEQS, BLOCK, COLS)...  65.7 us
    unnamed x1, local copies, waits for them, and re-layouts  1.87 us

profile of v5, /device:TPU:1, one launch (start us, length us, event | category | flops | bytes accessed | tf_op | source)
XLA Modules:
  0.0 67.5 jit_solution(1126007398056336006)
XLA Ops:
  0.0 65.7 %shard_map.91 = bf16[2,512,256]{2,1,0:T(8,128)(2,1)} custom-call(bf16[2,64,512]{2,1,0:T(8,128)(2,1)} %seq_hbm.1, f32[1024,128]{1,0:T(8,128)} %bitcast.6, f32[1,64]{1,0:T(1,128)} %bitcast.7, bf16[128,64]{1,0:T(8,128)(2,1)} %constant.8.clone.first_hbm, bf16[32,384]{1,0:T(8,128)(2,1)} %constant.9.clone.last_hbm, bf16[2,64,512]{2,1,0:T(8,128)(2,1)} %gate_hbm.1, ...), custom_call_target="tpu_custom_call" | custom-call | tf_op jit(solution)/shard_map/pallas_call | solution.py:452
  65.7 1.9 %copy.12 = bf16[2,512,256]{2,1,0:T(8,128)(2,1)} copy(bf16[2,512,256]{2,1,0:T(8,128)(2,1)} %shard_map.91) | data formatting | bytes 1048576
